TPU v7x, 32 devices: a whole 2x2x4 slice. The times are simulated.
32 devices in a mesh: dp: 4 (over z), seq: 8 (over y, x, core).
Axes of the slice: x: 2, y: 2, z: 4, core: 2. Of those that a mesh axis runs over, the one named last changes fastest.
Arguments:
- tokens: bfloat16 [4, 1024, 2048], P('dp', 'seq'), may hold values from -6 to 6
- segments: int32 [4, 1024], P('dp'), may hold values from 0 to 7, as said below
- exit_layer: int32 [4, 1024], P('dp', 'seq'), may hold values from 1 to 24, as said below
- first_gain: bfloat16 [2048], P(('dp', 'seq')), may hold values from 0.25 to 1.75
- first_shift: bfloat16 [2048], P(('dp', 'seq')), may hold values from -4 to 4
- query_weight: bfloat16 [2048, 2048], P(('dp', 'seq')), may hold values from -0.125 to 0.125
- query_bias: bfloat16 [2048], P(('dp', 'seq')), may hold values from -4 to 4
- key_weight: bfloat16 [2048, 2048], P(('dp', 'seq')), may hold values from -0.125 to 0.125
- value_weight: bfloat16 [2048, 2048], P(('dp', 'seq')), may hold values from -0.125 to 0.125
- value_bias: bfloat16 [2048], P(('dp', 'seq')), may hold values from -4 to 4
- output_weight: bfloat16 [2048, 2048], P(('dp', 'seq')), may hold values from -0.5 to 0.5
- output_bias: bfloat16 [2048], P(('dp', 'seq')), may hold values from -4 to 4
- second_gain: bfloat16 [2048], P(('dp', 'seq')), may hold values from 0.25 to 1.75
- second_shift: bfloat16 [2048], P(('dp', 'seq')), may hold values from -4 to 4
- up_weight: bfloat16 [2048, 8192], P(('dp', 'seq')), may hold values from -0.125 to 0.125
- up_bias: bfloat16 [8192], P(('dp', 'seq')), may hold values from -4 to 4
- down_weight: bfloat16 [8192, 2048], P(('dp', 'seq')), may hold values from -0.09375 to 0.09375
- down_bias: bfloat16 [2048], P(('dp', 'seq')), may hold values from -4 to 4
- cotangent: bfloat16 [4, 1024, 2048], P('dp', 'seq'), may hold values from -8 to 8
Outputs:
- layer_out: bfloat16 [4, 1024, 2048], P('dp', 'seq')
- tokens_gradient: bfloat16 [4, 1024, 2048], P('dp', 'seq')
- first_gain_gradient: float32 [2048], P(('dp', 'seq'))
- first_shift_gradient: float32 [2048], P(('dp', 'seq'))
- query_weight_gradient: float32 [2048, 2048], P(('dp', 'seq'))
- query_bias_gradient: float32 [2048], P(('dp', 'seq'))
- key_weight_gradient: float32 [2048, 2048], P(('dp', 'seq'))
- value_weight_gradient: float32 [2048, 2048], P(('dp', 'seq'))
- value_bias_gradient: float32 [2048], P(('dp', 'seq'))
- output_weight_gradient: float32 [2048, 2048], P(('dp', 'seq'))
- output_bias_gradient: float32 [2048], P(('dp', 'seq'))
- second_gain_gradient: float32 [2048], P(('dp', 'seq'))
- second_shift_gradient: float32 [2048], P(('dp', 'seq'))
- up_weight_gradient: float32 [2048, 8192], P(('dp', 'seq'))
- up_bias_gradient: float32 [8192], P(('dp', 'seq'))
- down_weight_gradient: float32 [8192, 2048], P(('dp', 'seq'))
- down_bias_gradient: float32 [2048], P(('dp', 'seq'))
Inputs may be any that keep to these rules, and one draw needn't show every extreme that they name: `segments`: in each sequence the document numbers start at 0, never fall, and every one of the 8 documents holds at least one position; one document of each sequence starts within the first 128 positions and ends within the last 128. `exit_layer`: within each document the exit layers never rise, so the tokens that exceed 12 form a prefix of the document; the first token of every document exceeds 12, and all tokens of the document that spans the sequence do.
All inputs are finite; a program needn't handle non-finite values.
Results may differ from a plain program's by a relative error of at most 0.03.
Values may be sent and summed in bfloat16 or wider, within the bound.
A program may use at most 576 MiB of HBM per device.

v0:
```python
import math

import jax
import jax.numpy as jnp
from jax import lax
from jax.sharding import PartitionSpec as P

HEADS = 32
LAYER = 12


EPS = 1e-05
NEG = -1e30


def activate(value):
    return jax.nn.gelu(value, approximate=True)


def layer_norm(value, gain, shift):
    mean = jnp.mean(value, axis=-1, keepdims=True)
    centred = value - mean
    spread = jnp.mean(centred * centred, axis=-1, keepdims=True)
    return centred * lax.rsqrt(spread + EPS) * gain + shift


def transposed(left, right):
    return lax.dot_general(
        left, right, (((1,), (1,)), ((), ())), preferred_element_type=jnp.float32
    )


def leading(left, right):
    return lax.dot_general(
        left, right, (((0,), (0,)), ((), ())), preferred_element_type=jnp.float32
    )


def visible(query_seg, query_pos, key_seg, key_pos):
    same = query_seg[:, :, None] == key_seg[:, None, :]
    return jnp.logical_and(same, key_pos[None, None, :] <= query_pos[None, :, None])


def by_blocks(step, carry, piece):
    length = jax.tree.leaves(piece)[0].shape[1]
    size = math.gcd(length, 128)

    def one(index, state):
        offset = index * size
        block = jax.tree.map(lambda part: lax.dynamic_slice_in_dim(part, offset, size, 1), piece)
        return step(state, block, offset)

    return lax.fori_loop(0, length // size, one, carry)


def on_device(
    tokens,
    segments,
    exit_layer,
    first_gain,
    first_shift,
    query_weight,
    query_bias,
    key_weight,
    value_weight,
    value_bias,
    output_weight,
    output_bias,
    second_gain,
    second_shift,
    up_weight,
    up_bias,
    down_weight,
    down_bias,
    cotangent,
):
    nseq, piece_len, width = tokens.shape
    head_count = HEADS
    head_size = width // head_count
    scale = head_size ** (-0.5)
    rows = nseq * piece_len
    own_first = lax.axis_index("seq") * piece_len
    own_pos = own_first + jnp.arange(piece_len, dtype=jnp.int32)
    own_seg = lax.dynamic_slice_in_dim(segments, own_first, piece_len, 1)
    keep = (exit_layer > LAYER).astype(jnp.float32).reshape(rows, 1)
    (
        gain_one,
        shift_one,
        query_full,
        query_shift,
        key_full,
        value_full,
        value_shift,
        output_full,
        output_shift,
        gain_two,
        shift_two,
        up_shift,
        down_shift,
    ) = (
        lax.all_gather(first_gain, ("dp", "seq"), axis=0, tiled=True),
        lax.all_gather(first_shift, ("dp", "seq"), axis=0, tiled=True),
        lax.all_gather(query_weight, ("dp", "seq"), axis=0, tiled=True),
        lax.all_gather(query_bias, ("dp", "seq"), axis=0, tiled=True),
        lax.all_gather(key_weight, ("dp", "seq"), axis=0, tiled=True),
        lax.all_gather(value_weight, ("dp", "seq"), axis=0, tiled=True),
        lax.all_gather(value_bias, ("dp", "seq"), axis=0, tiled=True),
        lax.all_gather(output_weight, ("dp", "seq"), axis=0, tiled=True),
        lax.all_gather(output_bias, ("dp", "seq"), axis=0, tiled=True),
        lax.all_gather(second_gain, ("dp", "seq"), axis=0, tiled=True),
        lax.all_gather(second_shift, ("dp", "seq"), axis=0, tiled=True),
        lax.all_gather(up_bias, ("dp", "seq"), axis=0, tiled=True),
        lax.all_gather(down_bias, ("dp", "seq"), axis=0, tiled=True),
    )
    gain_one = gain_one.astype(jnp.float32)
    shift_one = shift_one.astype(jnp.float32)
    gain_two = gain_two.astype(jnp.float32)
    shift_two = shift_two.astype(jnp.float32)
    inputs = tokens.astype(jnp.float32).reshape(rows, width)
    normed_one = layer_norm(inputs, gain_one, shift_one).astype(jnp.bfloat16)
    queries = (
        jnp.dot(normed_one, query_full, preferred_element_type=jnp.float32)
        + query_shift.astype(jnp.float32)
    ).astype(jnp.bfloat16)
    keys = jnp.dot(normed_one, key_full, preferred_element_type=jnp.float32).astype(jnp.bfloat16)
    values = (
        jnp.dot(normed_one, value_full, preferred_element_type=jnp.float32)
        + value_shift.astype(jnp.float32)
    ).astype(jnp.bfloat16)
    query_heads = queries.reshape(nseq, piece_len, head_count, head_size)
    key_heads = keys.reshape(nseq, piece_len, head_count, head_size)
    value_heads = values.reshape(nseq, piece_len, head_count, head_size)
    key_local = keys.reshape(nseq, piece_len, width)
    pair_local = jnp.concatenate([keys, values], axis=1).reshape(nseq, piece_len, 2 * width)

    def key_mask(start, length):
        key_pos = start + jnp.arange(length, dtype=jnp.int32)
        key_seg = lax.dynamic_slice_in_dim(segments, start, length, 1)
        return visible(own_seg, own_pos, key_seg, key_pos)[:, None]

    def local_scores(key_block):
        keyed = key_block.reshape(nseq, key_block.shape[1], head_count, head_size)
        return (
            jnp.einsum("sqhd,skhd->shqk", query_heads, keyed, preferred_element_type=jnp.float32)
            * scale
        )

    def norm_step(carry, block, start):
        top, total = carry
        allowed = key_mask(start, block.shape[1])
        scores = jnp.where(allowed, local_scores(block), NEG)
        new_top = jnp.maximum(top, jnp.max(scores, axis=-1))
        weights = jnp.where(allowed, jnp.exp(scores - new_top[..., None]), 0.0)
        return (new_top, total * jnp.exp(top - new_top) + jnp.sum(weights, axis=-1))

    start_norm = (
        jnp.full((nseq, head_count, piece_len), NEG, jnp.float32),
        jnp.zeros((nseq, head_count, piece_len), jnp.float32),
    )
    top, total = by_blocks(
        norm_step, start_norm, lax.all_gather(key_local, "seq", axis=1, tiled=True)
    )
    lse = top + jnp.log(total)

    def mix_step(acc, block, start):
        length = block.shape[1]
        allowed = key_mask(start, length)
        scores = local_scores(block[:, :, :width])
        probs = jnp.where(allowed, jnp.exp(scores - lse[..., None]), 0.0).astype(jnp.bfloat16)
        valued = block[:, :, width:].reshape(nseq, length, head_count, head_size)
        return acc + jnp.einsum(
            "shqk,skhd->sqhd", probs, valued, preferred_element_type=jnp.float32
        )

    empty_heads = jnp.zeros((nseq, piece_len, head_count, head_size), jnp.float32)
    mixed_heads = by_blocks(
        mix_step, empty_heads, lax.all_gather(pair_local, "seq", axis=1, tiled=True)
    )
    mixed = mixed_heads.reshape(rows, width).astype(jnp.bfloat16)
    attention = jnp.dot(
        mixed, output_full, preferred_element_type=jnp.float32
    ) + output_shift.astype(jnp.float32)
    middle = inputs + keep * attention
    normed_two = layer_norm(middle, gain_two, shift_two).astype(jnp.bfloat16)
    columns = normed_two
    before = jnp.dot(
        columns,
        lax.all_gather(up_weight, ("dp", "seq"), axis=0, tiled=True),
        preferred_element_type=jnp.float32,
    )
    pre_active = before + up_shift.astype(jnp.float32)
    hidden = activate(pre_active).astype(jnp.bfloat16)
    columns = hidden
    branch = jnp.dot(
        columns,
        lax.all_gather(down_weight, ("dp", "seq"), axis=0, tiled=True),
        preferred_element_type=jnp.float32,
    )
    branch = branch + down_shift.astype(jnp.float32)
    layer_out = (middle + keep * branch).astype(jnp.bfloat16).reshape(nseq, piece_len, width)
    upstream = cotangent.astype(jnp.float32).reshape(rows, width)
    branch_back = (keep * upstream).astype(jnp.bfloat16)
    down_shift_sum = jnp.sum(branch_back.astype(jnp.float32), axis=0)
    hidden_back = transposed(
        branch_back, lax.all_gather(down_weight, ("dp", "seq"), axis=0, tiled=True)
    )
    active_value, pull_active = jax.vjp(activate, pre_active)
    pre_back = pull_active(hidden_back)[0].astype(jnp.bfloat16)
    up_shift_sum = jnp.sum(pre_back.astype(jnp.float32), axis=0)
    down_gradient = lax.psum_scatter(
        leading(hidden, branch_back), ("dp", "seq"), scatter_dimension=0, tiled=True
    )
    normed_two_back = transposed(
        pre_back, lax.all_gather(up_weight, ("dp", "seq"), axis=0, tiled=True)
    )
    norm_result, pull_two = jax.vjp(layer_norm, middle, gain_two, shift_two)
    middle_part, gain_two_sum, shift_two_sum = pull_two(normed_two_back)
    middle_back = upstream + middle_part
    attention_back = (keep * middle_back).astype(jnp.bfloat16)
    output_shift_sum = jnp.sum(attention_back.astype(jnp.float32), axis=0)
    mixed_back = transposed(attention_back, output_full).astype(jnp.bfloat16)
    mixed_heads_back = mixed_back.reshape(nseq, piece_len, head_count, head_size)
    delta_rows = jnp.sum(mixed_heads_back.astype(jnp.float32) * mixed_heads, axis=-1)
    delta = delta_rows.transpose(0, 2, 1)
    lse_rows = lse.transpose(0, 2, 1)

    def query_step(acc, block, start):
        length = block.shape[1]
        allowed = key_mask(start, length)
        scores = local_scores(block[:, :, :width])
        probs = jnp.where(allowed, jnp.exp(scores - lse[..., None]), 0.0)
        valued = block[:, :, width:].reshape(nseq, length, head_count, head_size)
        keyed = block[:, :, :width].reshape(nseq, length, head_count, head_size)
        prob_back = jnp.einsum(
            "sqhd,skhd->shqk", mixed_heads_back, valued, preferred_element_type=jnp.float32
        )
        score_back = (probs * (prob_back - delta[..., None])).astype(jnp.bfloat16)
        return acc + jnp.einsum(
            "shqk,skhd->sqhd", score_back, keyed, preferred_element_type=jnp.float32
        )

    query_sum = by_blocks(
        query_step, empty_heads, lax.all_gather(pair_local, "seq", axis=1, tiled=True)
    )
    queries_back = (query_sum * scale).reshape(rows, width).astype(jnp.bfloat16)

    def key_step(carry, block, start):
        key_acc, value_acc = carry
        query_block, back_block, norm_block, delta_block = block
        length = query_block.shape[1]
        query_pos = start + jnp.arange(length, dtype=jnp.int32)
        query_seg = lax.dynamic_slice_in_dim(segments, start, length, 1)
        allowed = visible(query_seg, query_pos, own_seg, own_pos)[:, None]
        remote_query = query_block.astype(jnp.bfloat16).reshape(nseq, length, head_count, head_size)
        remote_back = back_block.astype(jnp.bfloat16).reshape(nseq, length, head_count, head_size)
        scores = (
            jnp.einsum(
                "sqhd,skhd->shqk", remote_query, key_heads, preferred_element_type=jnp.float32
            )
            * scale
        )
        probs = jnp.where(allowed, jnp.exp(scores - norm_block.transpose(0, 2, 1)[..., None]), 0.0)
        value_acc = value_acc + jnp.einsum(
            "shqk,sqhd->skhd",
            probs.astype(jnp.bfloat16),
            remote_back,
            preferred_element_type=jnp.float32,
        )
        prob_back = jnp.einsum(
            "sqhd,skhd->shqk", remote_back, value_heads, preferred_element_type=jnp.float32
        )
        score_back = (probs * (prob_back - delta_block.transpose(0, 2, 1)[..., None])).astype(
            jnp.bfloat16
        )
        key_acc = key_acc + jnp.einsum(
            "shqk,sqhd->skhd", score_back, remote_query, preferred_element_type=jnp.float32
        )
        return (key_acc, value_acc)

    query_send = queries.astype(jnp.float32).reshape(nseq, piece_len, width)
    back_send = mixed_back.astype(jnp.float32).reshape(nseq, piece_len, width)
    key_sum, value_sum = by_blocks(
        key_step,
        (empty_heads, empty_heads),
        (
            lax.all_gather(query_send.astype(jnp.bfloat16), "seq", axis=1, tiled=True).astype(
                jnp.float32
            ),
            lax.all_gather(back_send.astype(jnp.bfloat16), "seq", axis=1, tiled=True).astype(
                jnp.float32
            ),
            lax.all_gather(lse_rows.astype(jnp.bfloat16), "seq", axis=1, tiled=True).astype(
                jnp.float32
            ),
            lax.all_gather(delta_rows.astype(jnp.bfloat16), "seq", axis=1, tiled=True).astype(
                jnp.float32
            ),
        ),
    )
    keys_back = (key_sum * scale).reshape(rows, width).astype(jnp.bfloat16)
    values_back = value_sum.reshape(rows, width).astype(jnp.bfloat16)
    query_shift_sum = jnp.sum(queries_back.astype(jnp.float32), axis=0)
    value_shift_sum = jnp.sum(values_back.astype(jnp.float32), axis=0)
    normed_one_back = (
        transposed(queries_back, query_full)
        + transposed(keys_back, key_full)
        + transposed(values_back, value_full)
    )
    norm_first, pull_one = jax.vjp(layer_norm, inputs, gain_one, shift_one)
    inputs_part, gain_one_sum, shift_one_sum = pull_one(normed_one_back)
    tokens_gradient = (
        (middle_back + inputs_part).astype(jnp.bfloat16).reshape(nseq, piece_len, width)
    )
    stacked_back = jnp.concatenate([queries_back, keys_back, values_back], axis=1)
    row_gradient = lax.psum_scatter(
        jnp.concatenate(
            [
                leading(normed_one, stacked_back),
                leading(mixed, attention_back),
                leading(normed_two, pre_back),
            ],
            axis=1,
        ),
        ("dp", "seq"),
        scatter_dimension=0,
        tiled=True,
    )
    (
        gain_one_part,
        shift_one_part,
        query_shift_part,
        value_shift_part,
        output_shift_part,
        gain_two_part,
        shift_two_part,
        up_shift_part,
        down_shift_part,
    ) = (
        lax.psum_scatter(gain_one_sum, ("dp", "seq"), scatter_dimension=0, tiled=True),
        lax.psum_scatter(shift_one_sum, ("dp", "seq"), scatter_dimension=0, tiled=True),
        lax.psum_scatter(query_shift_sum, ("dp", "seq"), scatter_dimension=0, tiled=True),
        lax.psum_scatter(value_shift_sum, ("dp", "seq"), scatter_dimension=0, tiled=True),
        lax.psum_scatter(output_shift_sum, ("dp", "seq"), scatter_dimension=0, tiled=True),
        lax.psum_scatter(gain_two_sum, ("dp", "seq"), scatter_dimension=0, tiled=True),
        lax.psum_scatter(shift_two_sum, ("dp", "seq"), scatter_dimension=0, tiled=True),
        lax.psum_scatter(up_shift_sum, ("dp", "seq"), scatter_dimension=0, tiled=True),
        lax.psum_scatter(down_shift_sum, ("dp", "seq"), scatter_dimension=0, tiled=True),
    )
    return (
        layer_out,
        tokens_gradient,
        gain_one_part,
        shift_one_part,
        row_gradient[:, :width],
        query_shift_part,
        row_gradient[:, width : 2 * width],
        row_gradient[:, 2 * width : 3 * width],
        value_shift_part,
        row_gradient[:, 3 * width : 4 * width],
        output_shift_part,
        gain_two_part,
        shift_two_part,
        row_gradient[:, 4 * width :],
        up_shift_part,
        down_gradient,
        down_shift_part,
    )


def solution(mesh):
    placed = (
        P("dp", "seq", None),
        P("dp", None),
        P("dp", "seq"),
        P(("dp", "seq")),
        P(("dp", "seq")),
        P(("dp", "seq"), None),
        P(("dp", "seq")),
        P(("dp", "seq"), None),
        P(("dp", "seq"), None),
        P(("dp", "seq")),
        P(("dp", "seq"), None),
        P(("dp", "seq")),
        P(("dp", "seq")),
        P(("dp", "seq")),
        P(("dp", "seq"), None),
        P(("dp", "seq")),
        P(("dp", "seq"), None),
        P(("dp", "seq")),
        P("dp", "seq", None),
    )
    return jax.shard_map(
        on_device,
        mesh=mesh,
        in_specs=placed,
        out_specs=(
            P("dp", "seq", None),
            P("dp", "seq", None),
            P(("dp", "seq")),
            P(("dp", "seq")),
            P(("dp", "seq"), None),
            P(("dp", "seq")),
            P(("dp", "seq"), None),
            P(("dp", "seq"), None),
            P(("dp", "seq")),
            P(("dp", "seq"), None),
            P(("dp", "seq")),
            P(("dp", "seq")),
            P(("dp", "seq")),
            P(("dp", "seq"), None),
            P(("dp", "seq")),
            P(("dp", "seq"), None),
            P(("dp", "seq")),
        ),
        check_vma=False,
    )
```

profile of v0, /device:TPU:0, one launch (start us, length us, event | category | flops | bytes accessed | tf_op | source)
XLA Modules:
  0.0 3804.1 jit_solution(7685401220206984824)
XLA Ops:
  16.2 43.0 %all-reduce.19 = (bf16[2048]{0:T(1024)(128)(2,1)S(1)}, bf16[2048]{0:T(1024)(128)(2,1)S(1)}, bf16[2048]{0:T(1024)(128)(2,1)S(1)}, bf16[2048]{0:T(1024)(128)(2,1)S...) all-reduce(bf16[2048]{0:T(1024)(128)(2,1)S(1)} %dynamic-update-slic, ...), channel_id=1, replica_groups=mesh['dp'=4,'seq'=8] {'dp','seq'}, use_global_device_ids=true, to_apply=%add.2 | all-reduce | flops 16384 | bytes 65536
  61.9 29.3 all-gather.16.cloned.1.call-done
  91.2 5.7 convolution_convert_fusion.1
  97.0 73.1 %all-gather.18.cloned.1.call-done = bf16[2048,2048]{1,0:T(8,128)(2,1)} async-done(((bf16[64,2048]{1,0:T(8,128)(2,1)}), bf16[2048,2048]{1,0:T(8,128)(2,1)}) %all-gather.18.cloned.1.call-update) | async-done | bytes 8388624 | tf_op jit(solution)/shard_map/all_gather | solution.py:106
  170.1 4.7 fusion.59
  178.2 39.2 %all-gather.4 = bf16[32,1,256]{2,1,0:T(2,128)(2,1)S(1)} all-gather(bf16[1,1,256]{2,1,0:T(2,128)(2,1)S(1)} %reshape.788), channel_id=1, replica_groups=mesh['dp'=4,'seq'=8] {'dp','seq'}, dimensions={0}, use_global_device_ids=true | all-gather | bytes 16896 | tf_op jit(solution)/shard_map/all_gather | solution.py:112
  219.5 29.4 all-gather.20.cloned.1.call-done
  248.9 4.7 fusion.60
  254.5 32.1 all-gather.30.cloned.1.call-done
  286.6 21.5 while.60
  308.1 9.0 all_gather.84
  317.1 26.2 all-gather.28.cloned.1.call-done
  343.3 12.0 copy.63
  355.3 19.6 while.61
  377.2 46.3 %all-gather.22.cloned.1.call-done = bf16[2048,2048]{1,0:T(8,128)(2,1)} async-done(((bf16[64,2048]{1,0:T(8,128)(2,1)}), bf16[2048,2048]{1,0:T(8,128)(2,1)}) %all-gather.22.cloned.1.call-update) | async-done | bytes 8388624 | tf_op jit(solution)/shard_map/all_gather | solution.py:108
  423.5 4.8 fusion.102
  428.6 191.2 %all-gather.24.cloned.1.call-done = bf16[2048,8192]{1,0:T(8,128)(2,1)} async-done(((bf16[64,8192]{1,0:T(8,128)(2,1)}), bf16[2048,8192]{1,0:T(8,128)(2,1)}) %all-gather.24.cloned.1.call-update) | async-done | bytes 33554448 | tf_op jit(solution)/shard_map/all_gather | solution.py:188
  619.8 17.9 convolution_add_fusion
  637.7 177.9 %all-gather.26.cloned.1.call-done = bf16[8192,2048]{1,0:T(8,128)(2,1)} async-done(((bf16[256,2048]{1,0:T(8,128)(2,1)}), bf16[8192,2048]{1,0:T(8,128)(2,1)}) %all-gather.26.cloned.1.call-update) | async-done | bytes 33554448 | tf_op jit(solution)/shard_map/all_gather | solution.py:196
  815.6 19.6 convert_reduce_fusion
  835.2 18.3 multiply_reduce_fusion
  856.1 6.5 convolution_convert_fusion
  864.9 50.5 %while.62 = (s32[]{:T(128)}, f32[1,128,32,64]{1,3,2,0:T(8,128)}, bf16[1,1024,4096]{1,2,0:T(8,128)(2,1)}, s32[1,128]{1,0:T(1,128)S(1)}, s32[1,1024]{1,0:T(1,128)S...) while((s32[]{:T(128)}, f32[1,128,32,64]{1,3,2,0:T(8,128)}, ...), condition=%wide.region_14.15_spmd.clone, body=%wide.region_13.14_spmd.clone.sunk | while | flops 205046016 | bytes 11079917 | solution.py:53
  873.7 3.6 fusion.175
  880.0 3.6 fusion.175
  886.4 3.6 fusion.175
  892.7 3.7 fusion.175
  899.1 3.6 fusion.175
  905.4 3.6 fusion.175
  911.8 3.6 fusion.175
  917.8 8.9 all_gather.86
  926.8 7.4 fusion.103
  934.2 8.1 fusion.104
  942.2 23.4 fusion.94
  965.6 79.2 %while.63 = (s32[]{:T(128)}, f32[1,128,32,64]{1,3,2,0:T(8,128)}, f32[1,128,32,64]{1,3,2,0:T(8,128)}, bf16[1,1024,2048]{2,1,0:T(8,128)(2,1)}, s32[1,1024]{1,0:T(1...) while((s32[]{:T(128)}, f32[1,128,32,64]{1,3,2,0:T(8,128)}, ...), condition=%wide.region_16.17_spmd.clone, body=%wide.region_15.16_spmd.clone.sunk | while | flops 273203456 | bytes 17961192 | solution.py:53
  978.2 3.4 fusion.184
  998.4 3.4 fusion.184
  1008.5 3.4 fusion.184
  1018.6 3.4 fusion.184
  1047.4 20.7 fusion.63
  1068.1 6.3 convolution_add_fusion.3
  1074.5 7.0 fusion.99
  1082.7 87.1 %pad_maximum_fusion = f32[2048,16384]{1,0:T(8,128)} fusion(f32[2048,8192]{1,0:T(8,128)} %fusion.94, f32[2048,2048]{1,0:T(8,128)} %fusion.104, f32[2048,6144]{1,0:T(8,128)} %fusion.63), kind=kLoop, calls=%fused_computation.78 | loop fusion | flops 67108864 | bytes 268435456 | tf_op jit(solution)/shard_map/concatenate | solution.py:316
  1170.8 25.7 fusion.87
  1197.8 17.9 fusion.62
  1228.5 1863.9 %all-reduce.23.cloned.1.call-done = f32[2048,16384]{1,0:T(8,128)} async-done(((f32[2048,16384]{1,0:T(8,128)}), f32[2048,16384]{1,0:T(8,128)}) %all-reduce.23.cloned.1.call-update) | async-done | bytes 134217744
  3092.4 3.5 dynamic-slice.18
  3099.2 698.2 %reduce-scatter.2.cloned.1.call-done = f32[256,2048]{1,0:T(8,128)} async-done(((f32[8192,2048]{1,0:T(8,128)}), f32[256,2048]{1,0:T(8,128)}) %reduce-scatter.2.cloned.1.call-update) | async-done | bytes 2097168 | tf_op jit(solution)/shard_map/reduce_scatter | solution.py:210
  (426 shorter events, 179.6 us)
Async XLA Ops:
  7.2 84.0 %all-gather.16.cloned.1.call-start = ((), (), s32[]{:S(2)}) async-start(), calls=%async_computation.1 | async-start | bytes 8650752 | tf_op jit(solution)/shard_map/all_gather | solution.py:105
  7.9 162.2 %all-gather.18.cloned.1.call-start = ((), (), s32[]{:S(2)}) async-start(), calls=%async_computation.2 | async-start | bytes 8650752 | tf_op jit(solution)/shard_map/all_gather | solution.py:106
  8.7 240.3 %all-gather.20.cloned.1.call-start = ((), (), s32[]{:S(2)}) async-start(), calls=%async_computation.3 | async-start | bytes 8650752 | tf_op jit(solution)/shard_map/all_gather | solution.py:103
  9.4 277.2 %all-gather.30.cloned.1.call-start = ((), (), s32[]{:S(2)}) async-start(), calls=%async_computation.9 | async-start | bytes 4718592 | tf_op jit(solution)/shard_map/all_gather | solution.py:161
  59.2 1022.3 %copy-start.24 = (f32[2048]{0:T(1024)}, f32[2048]{0:T(1024)S(1)}, u32[]{:S(2)}) copy-start(f32[2048]{0:T(1024)S(1)} %convert_element_type.208) | copy-start | bytes 24580
  60.4 1021.1 %copy-start.26 = (f32[128]{0:T(128)}, f32[128]{0:T(128)S(1)}, u32[]{:S(2)}) copy-start(f32[128]{0:T(128)S(1)} %broadcast_multiply_fusion.1) | copy-start | bytes 1540
  61.9 35.0 copy-start.38
  61.9 1019.7 %copy-start.28 = (f32[128]{0:T(128)}, f32[128]{0:T(128)S(1)}, u32[]{:S(2)}) copy-start(f32[128]{0:T(128)S(1)} %fusion.84) | copy-start | bytes 1540
  61.9 108.2 %copy-start.3 = (bf16[1,128,2048]{2,1,0:T(8,128)(2,1)S(1)}, bf16[1,128,2048]{2,1,0:T(8,128)(2,1)}, u32[]{:S(2)}) copy-start(bf16[1,128,2048]{2,1,0:T(8,128)(2,1)} %param.27) | copy-start | bytes 1572868
  96.9 246.4 %all-gather.28.cloned.1.call-start = ((), (), s32[]{:S(2)}) async-start(), calls=%async_computation.8 | async-start | bytes 9437184 | tf_op jit(solution)/shard_map/all_gather | solution.py:177
  97.0 77.9 %copy-start.19 = (bf16[128,2048]{1,0:T(8,128)(2,1)S(1)}, bf16[128,2048]{1,0:T(8,128)(2,1)}, u32[]{:S(2)}) copy-start(bf16[128,2048]{1,0:T(8,128)(2,1)} %convolution_convert_fusion.1) | copy-start | bytes 1572868
  174.8 3.3 copy-start.41
  174.9 42.6 %copy-start.40 = (s32[1,1024]{1,0:T(1,128)S(1)}, s32[1,1024]{1,0:T(1,128)}, u32[]{:S(2)}) copy-start(s32[1,1024]{1,0:T(1,128)} %param.28) | copy-start | bytes 12292
  174.9 42.6 %copy-start.42 = (s32[1,128]{1,0:T(1,128)S(1)}, s32[1,128]{1,0:T(1,128)}, u32[]{:S(2)}) copy-start(s32[1,128]{1,0:T(1,128)} %param.29) | copy-start | bytes 1540
  175.9 247.6 %all-gather.22.cloned.1.call-start = ((), (), s32[]{:S(2)}) async-start(), calls=%async_computation.4 | async-start | bytes 8650752 | tf_op jit(solution)/shard_map/all_gather | solution.py:108
  176.5 443.3 %all-gather.24.cloned.1.call-start = ((), (), s32[]{:S(2)}) async-start(), calls=%async_computation.5 | async-start | bytes 34603008 | tf_op jit(solution)/shard_map/all_gather | solution.py:188
  177.3 638.4 %all-gather.26.cloned.1.call-start = ((), (), s32[]{:S(2)}) async-start(), calls=%async_computation.6 | async-start | bytes 34603008 | tf_op jit(solution)/shard_map/all_gather | solution.py:196
  178.0 787.6 %all-gather.32.cloned.1.call-start = ((), (), s32[]{:S(2)}) async-start(), calls=%async_computation.10 | async-start | bytes 4718592 | tf_op jit(solution)/shard_map/all_gather | solution.py:286
  217.5 636.5 %copy-start.30 = (f32[128]{0:T(128)}, f32[128]{0:T(128)S(1)}, u32[]{:S(2)}) copy-start(f32[128]{0:T(128)S(1)} %fusion.83) | copy-start | bytes 1540
  254.4 711.2 %all-gather.34.cloned.1.call-start = ((), (), s32[]{:S(2)}) async-start(), calls=%async_computation.11 | async-start | bytes 4718592 | tf_op jit(solution)/shard_map/all_gather | solution.py:289
  377.2 51.1 %copy-start.11 = (bf16[1,128,32,64]{1,3,2,0:T(8,128)(2,1)}, bf16[1,128,32,64]{1,3,2,0:T(8,128)(2,1)S(1)}, u32[]{:S(2)}) copy-start(bf16[1,128,32,64]{1,3,2,0:T(8,128)(2,1)S(1)} %convert_element_type.216) | copy-start | bytes 1572868
  428.3 425.3 %copy-start = (f32[128,2048]{1,0:T(8,128)}, f32[128,2048]{1,0:T(8,128)S(1)}, u32[]{:S(2)}) copy-start(f32[128,2048]{1,0:T(8,128)S(1)} %get-tuple-element.1057) | copy-start | bytes 3145732
  619.8 195.8 %copy-start.14 = (bf16[1,128,2048]{2,1,0:T(8,128)(2,1)S(1)}, bf16[1,128,2048]{2,1,0:T(8,128)(2,1)}, u32[]{:S(2)}) copy-start(bf16[1,128,2048]{2,1,0:T(8,128)(2,1)} %param.45) | copy-start | bytes 1572868
  854.0 8.6 copy-start.35
  856.1 6.5 copy-start.17
  856.1 7.6 copy-start.21
  863.6 353.5 %all-reduce.25.cloned.1.call-start = ((), (), s32[]{:S(2)}) async-start(), calls=%async_computation.13 | async-start | bytes 196608
  917.0 17.1 copy-start.13
  926.8 7.4 copy-start.12
  926.8 7.4 copy-start.18
  934.2 8.1 copy-start.1
  934.2 8.1 copy-start.6
  1047.4 20.7 copy-start.22
  1068.1 6.4 copy-start.4
  1074.5 7.1 copy-start.39
  1081.5 88.2 %copy-start.33 = (f32[128]{0:T(128)}, f32[128]{0:T(128)S(1)}, u32[]{:S(2)}) copy-start(f32[128]{0:T(128)S(1)} %multiply_multiply_fusion.2) | copy-start | bytes 1540
  1082.7 2009.7 %all-reduce.23.cloned.1.call-start = ((), (), s32[]{:S(2)}) async-start(), calls=%async_computation.12 | async-start | bytes 268435456
  1169.8 2627.6 %reduce-scatter.2.cloned.1.call-start = ((), (), s32[]{:S(2)}) async-start(), calls=%async_computation.7 | async-start | bytes 69206016 | tf_op jit(solution)/shard_map/reduce_scatter | solution.py:210
  1196.5 1.2 copy-start.2
  1197.7 18.0 copy-start.37
  1197.7 18.0 copy-start.5
  1197.7 18.0 copy-start.8
  1197.7 18.0 copy-start.10
  1197.7 18.0 copy-start.25
  1197.8 18.0 copy-start.27
  1197.8 18.0 copy-start.29
  1197.8 18.0 copy-start.34
  1197.8 18.0 copy-start.36
  (8 other events, 7.6 us)
Sparse Core Ops, SparseCore 0:
  10.9 80.2 all-gather.15
  94.0 76.0 all-gather.17
  173.0 75.8 all-gather.19
  251.2 35.2 all-gather.29
  288.9 54.3 all-gather.27
  346.0 77.4 all-gather.21
  426.4 193.3 all-gather.23
  622.6 192.9 all-gather.25
  818.1 34.8 all-gather.31
  863.7 34.6 all-gather.33
  1082.8 123.3 all-reduce.24
  1213.6 1878.7 all-reduce.22
  3095.4 701.8 reduce-scatter.1
where the time goes:
time: 3820 us; the launch traced here: 3800 us
  waiting for transfers between devices  3170 us (83%)
  matrix products  307 us (8%)
  other arithmetic  109 us (3%)
  blocking collectives  100 us (3%)
  local copies, waits for them, and re-layouts  99.3 us (3%)
    unnamed x15, waiting for transfers between devices  1870 us
    reduce_scatter x1, waiting for transfers between devices, on_device(): lax.psum_scatter(leading(hidden, branch_back), ('dp', 'seq'), scatter_dim...  698 us
    all_gather x1, waiting for transfers between devices, on_device(): lax.all_gather(up_weight, ('dp', 'seq'), axis=0, tiled=True)  191 us
    all_gather x1, waiting for transfers between devices, on_device(): lax.all_gather(down_weight, ('dp', 'seq'), axis=0, tiled=True)  178 us
    concatenate x1, other arithmetic, on_device(): jnp.concatenate([leading(normed_one, stacked_back), leading(mixed, attent...  87.1 us
    dot_general x4, matrix products, leading(): lax.dot_general(left, right, (((0,), (0,)), ((), ())), preferred_element_...  77.8 us
  transfers between devices with their start and end apart: 13, of which 10 were waited for; matrix products, arithmetic and copies ran while one was open for 10% of the time, Pallas kernels for 0%

commit v1 on v0

--- a/solution.py
+++ b/solution.py
@@ -1,8 +1,11 @@
+import functools
 import math
 
 import jax
 import jax.numpy as jnp
 from jax import lax
+from jax.experimental import pallas as pl
+from jax.experimental.pallas import tpu as pltpu
 from jax.sharding import PartitionSpec as P
 
 HEADS = 32
@@ -367,6 +370,631 @@
     )
 
 
+MESH = pl.DeviceIdType.MESH
+ORDERS = ("xyz", "yzx", "zxy")
+CANON = "zyx"
+
+def place():
+    d = lax.axis_index("dp"); s = lax.axis_index("seq")
+    half = lax.axis_size("dp") // 2
+    far = d // half
+    z = d + far * (2 * half - 1 - 2 * d)
+    return dict(d=d, s=s, g=far, z=z, y=s // 4, x=(s // 2) % 2, c=s % 2)
+
+def beside(w, dim):
+    if dim == "z":
+        return (w["d"] + 1 - 2 * (w["d"] % 2), w["s"])
+    step = {"c": 1, "x": 2, "y": 4}[dim]
+    return (w["d"], w["s"] + step * (1 - 2 * w[dim]))
+
+def greet(ids):
+    bar = pltpu.get_barrier_semaphore()
+    for i in ids:
+        pl.semaphore_signal(bar, inc=1, device_id=i, device_id_type=MESH)
+    pl.semaphore_wait(bar, len(ids))
+
+def column_parts(width):
+    unit = width // 128
+    cuts = [unit - 2 * (unit // 3), unit // 3, unit // 3]
+    out, at = [], 0
+    for c in cuts:
+        out.append(pl.ds(at * 128, c * 128)); at += c
+    return out
+
+def box(w, open_dims, other=()):
+    return tuple(pl.ds(0, 2) if q in open_dims else (1 - w[q] if q in other else w[q]) for q in CANON)
+
+def gather_kernel(src, out, send, recv, csend, crecv, lsem):
+    w = place()
+    rows = src.shape[0]
+    parts = column_parts(src.shape[1])
+    greet([beside(w, q) for q in "cxyz"])
+    def remote(a, b, ss, rs, dim):
+        return pltpu.make_async_remote_copy(src_ref=a, dst_ref=b, send_sem=ss, recv_sem=rs, device_id=beside(w, dim), device_id_type=MESH)
+    own = (w["z"], w["y"], w["x"], w["c"])
+    everything = []
+    links = {}
+    for p, cols in enumerate(parts):
+        cp = remote(src.at[:, cols], out.at[own + (slice(None), cols)], send.at[p, 0], recv.at[p, 0], ORDERS[p][0])
+        cp.start(); links[p, 0] = cp
+    keep = pltpu.make_async_copy(src, out.at[own], lsem)
+    keep.start()
+    sides = []
+    for p, cols in enumerate(parts):
+        cp = remote(src.at[:, cols], out.at[own + (slice(None), cols)], csend.at[p, 0], crecv.at[p, 0], "c")
+        cp.start(); sides.append(cp)
+    keep.wait()
+    for k in range(3):
+        for p, cols in enumerate(parts):
+            order = ORDERS[p]
+            links[p, k].wait_recv()
+            if k < 2:
+                at = box(w, order[: k + 1]) + (w["c"], slice(None), cols)
+                cp = remote(out.at[at], out.at[at], send.at[p, k + 1], recv.at[p, k + 1], order[k + 1])
+                cp.start(); links[p, k + 1] = cp
+            at = box(w, order[:k], order[k]) + (w["c"], slice(None), cols)
+            cp = remote(out.at[at], out.at[at], csend.at[p, k + 1], crecv.at[p, k + 1], "c")
+            cp.start(); sides.append(cp)
+    for cp in links.values():
+        cp.wait_send()
+    for cp in sides:
+        cp.wait()
+
+def cube_gather(own, name, cid):
+    rows, width = own.shape
+    return pl.pallas_call(
+        gather_kernel,
+        out_shape=jax.ShapeDtypeStruct((2, 2, 2, 2, rows, width), own.dtype),
+        in_specs=[pl.BlockSpec(memory_space=pltpu.VMEM)],
+        out_specs=pl.BlockSpec(memory_space=pltpu.VMEM),
+        scratch_shapes=[pltpu.SemaphoreType.DMA((3, 3)), pltpu.SemaphoreType.DMA((3, 3)), pltpu.SemaphoreType.DMA((3, 4)), pltpu.SemaphoreType.DMA((3, 4)), pltpu.SemaphoreType.DMA],
+        compiler_params=pltpu.CompilerParams(collective_id=cid, has_side_effects=True, vmem_limit_bytes=40 << 20),
+        name=name,
+    )(own)
+
+def scatter_kernel(src, out, acc, side, r0, r1, r2, send, recv, csend, crecv, lsem):
+    w = place()
+    rows, width = out.shape
+    parts = column_parts(width)
+    greet([beside(w, q) for q in "cxyz"])
+    def remote(a, b, ss, rs, dim):
+        return pltpu.make_async_remote_copy(src_ref=a, dst_ref=b, send_sem=ss, recv_sem=rs, device_id=beside(w, dim), device_id_type=MESH)
+    alls = (pl.ds(0, 2),) * 3
+    first, local = [], []
+    for p, cols in enumerate(parts):
+        cp = remote(src.at[alls + (1 - w["c"], slice(None), cols)], side.at[alls + (slice(None), cols)], csend.at[p], crecv.at[p], "c")
+        cp.start(); first.append(cp)
+        lc = pltpu.make_async_copy(src.at[alls + (w["c"], slice(None), cols)], acc.at[alls + (slice(None), cols)], lsem.at[p])
+        lc.start(); local.append(lc)
+    land = (r0, r1, r2)
+    def coords(order, k, fixed_k, a, b):
+        left = [q for q in CANON if q in order[k + 1:]]
+        vals = dict(zip(left, (a, b)))
+        return tuple(vals[q] if q in vals else (w[q] if q != order[k] else (w[q] if fixed_k else 1 - w[q])) for q in CANON)
+    links = {}
+    def add_side(p, cols, fixed):
+        order = ORDERS[p]
+        @pl.loop(0, 4)
+        def _(i):
+            at = coords(order, 0, fixed, i // 2, i % 2) + (slice(None), cols)
+            acc[at] = (acc[at].astype(jnp.float32) + side[at].astype(jnp.float32)).astype(acc.dtype)
+    def push(p, cols, k):
+        order = ORDERS[p]
+        at = box(w, order[k + 1:], order[k]) + (slice(None), cols)
+        n = 2 - k
+        width_p = cols.size
+        dst = land[k].at[(p,) + (pl.ds(0, 2),) * n + (slice(None), pl.ds(0, width_p))]
+        cp = remote(acc.at[at], dst, send.at[p, k], recv.at[p, k], order[k])
+        cp.start(); links[p, k] = cp
+    for p, cols in enumerate(parts):
+        first[p].wait_recv(); local[p].wait()
+        add_side(p, cols, False)
+        push(p, cols, 0)
+        add_side(p, cols, True)
+    for k in range(2):
+        for p, cols in enumerate(parts):
+            order = ORDERS[p]
+            links[p, k].wait_recv()
+            left = [q for q in CANON if q in order[k + 1:]]
+            nxt = left.index(order[k + 1])
+            def add(other):
+                val = (1 - w[order[k + 1]]) if other else w[order[k + 1]]
+                if k == 0:
+                    @pl.loop(0, 2)
+                    def _(i):
+                        ab = (val, i) if nxt == 0 else (i, val)
+                        at = coords(order, 0, True, *ab) + (slice(None), cols)
+                        got = r0[(p,) + ab + (slice(None), pl.ds(0, cols.size))]
+                        acc[at] = (acc[at].astype(jnp.float32) + got.astype(jnp.float32)).astype(acc.dtype)
+                else:
+                    at = coords(order, 1, True, val, val) + (slice(None), cols)
+                    got = r1[(p, val, slice(None), pl.ds(0, cols.size))]
+                    acc[at] = (acc[at].astype(jnp.float32) + got.astype(jnp.float32)).astype(acc.dtype)
+            add(True)
+            push(p, cols, k + 1)
+            add(False)
+    own = (w["z"], w["y"], w["x"])
+    for p, cols in enumerate(parts):
+        links[p, 2].wait_recv()
+        out[:, cols] = acc[own + (slice(None), cols)].astype(jnp.float32) + r2[p, :, pl.ds(0, cols.size)].astype(jnp.float32)
+    for cp in links.values():
+        cp.wait_send()
+    for cp in first:
+        cp.wait_send()
+
+def cube_scatter(partial, name, cid):
+    rows, width = partial.shape[-2:]
+    most = column_parts(width)[0].size
+    dt = partial.dtype
+    return pl.pallas_call(
+        scatter_kernel,
+        out_shape=jax.ShapeDtypeStruct((rows, width), jnp.float32),
+        in_specs=[pl.BlockSpec(memory_space=pl.ANY)],
+        out_specs=pl.BlockSpec(memory_space=pltpu.VMEM),
+        scratch_shapes=[pltpu.VMEM((2, 2, 2, rows, width), dt), pltpu.VMEM((2, 2, 2, rows, width), dt),
+            pltpu.VMEM((3, 2, 2, rows, most), dt), pltpu.VMEM((3, 2, rows, most), dt), pltpu.VMEM((3, rows, most), dt),
+            pltpu.SemaphoreType.DMA((3, 3)), pltpu.SemaphoreType.DMA((3, 3)), pltpu.SemaphoreType.DMA((3,)), pltpu.SemaphoreType.DMA((3,)), pltpu.SemaphoreType.DMA((3,))],
+        compiler_params=pltpu.CompilerParams(collective_id=cid, has_side_effects=True, vmem_limit_bytes=40 << 20),
+        name=name,
+    )(partial)
+
+def peer(w, r):
+    n = lax.axis_size("seq")
+    e, s = r // n, r % n
+    return (e + w["g"] * (lax.axis_size("dp") - 1 - 2 * e), s)
+
+def anyone(w, i):
+    n = lax.axis_size("seq")
+    return (i // n, i % n)
+
+def swap_kernel(device_of, row, src, out, send, recv, lsem):
+    w = place()
+    n = src.shape[0]
+    me = w[row] * lax.axis_size("seq") + w["s"]
+    others = [(me + k) % n for k in range(1, n)]
+    greet([device_of(w, r) for r in others])
+    cps = []
+    for k, r in enumerate(others):
+        cp = pltpu.make_async_remote_copy(src_ref=src.at[r], dst_ref=out.at[me], send_sem=send.at[k], recv_sem=recv.at[k], device_id=device_of(w, r), device_id_type=MESH)
+        cp.start(); cps.append(cp)
+    lc = pltpu.make_async_copy(src.at[me], out.at[me], lsem)
+    lc.start(); lc.wait()
+    for cp in cps:
+        cp.wait()
+
+def group_swap(blocks, name, cid):
+    return swap(peer, "z", blocks, name, cid)
+
+
+def world_swap(blocks, name, cid):
+    return swap(anyone, "d", blocks, name, cid)
+
+
+def swap(device_of, row, blocks, name, cid):
+    n = blocks.shape[0]
+    return pl.pallas_call(
+        functools.partial(swap_kernel, device_of, row),
+        out_shape=jax.ShapeDtypeStruct(blocks.shape, blocks.dtype),
+        in_specs=[pl.BlockSpec(memory_space=pl.ANY)],
+        out_specs=pl.BlockSpec(memory_space=pl.ANY),
+        scratch_shapes=[pltpu.SemaphoreType.DMA((n - 1,)), pltpu.SemaphoreType.DMA((n - 1,)), pltpu.SemaphoreType.DMA],
+        compiler_params=pltpu.CompilerParams(collective_id=cid, has_side_effects=True),
+        name=name,
+    )(blocks)
+
+
+def head_lanes(width, head, size):
+    lane = lax.broadcasted_iota(jnp.int32, (1, width), 1)
+    return jnp.logical_and(lane >= head * size, lane < (head + 1) * size)
+
+
+def used_pairs(key_seg, query_seg, first, length, block):
+    key_pos = lax.broadcasted_iota(jnp.int32, (length, 1), 0)
+    query_pos = first + lax.broadcasted_iota(jnp.int32, (1, block), 1)
+    return jnp.logical_and(key_seg == query_seg, key_pos <= query_pos)
+
+
+def across(left, right):
+    return lax.dot_general(
+        left, right, (((1,), (1,)), ((), ())), preferred_element_type=jnp.float32
+    )
+
+
+def attend_kernel(size, block, q_ref, k_ref, v_ref, key_seg_ref, query_seg_ref, mixed_ref, lse_ref):
+    length, width = q_ref.shape[1:]
+    heads = width // size
+    scale = size**-0.5
+    flipped = v_ref[0].T
+    for first in range(0, length, block):
+        upto = first + block
+        rows = pl.ds(first, block)
+        allowed = used_pairs(
+            key_seg_ref[0, pl.ds(0, upto), :], query_seg_ref[0, :, rows], first, upto, block
+        )
+        keys = k_ref[0, pl.ds(0, upto), :]
+        query = q_ref[0, rows, :] * jnp.asarray(scale, jnp.bfloat16)
+        parts = []
+        for head in range(heads):
+            own = jnp.where(head_lanes(width, head, size), query, jnp.zeros_like(query))
+            scores = jnp.where(allowed, across(keys, own), NEG)
+            top = jnp.max(scores, axis=0, keepdims=True)
+            weights = jnp.exp(scores - top)
+            total = jnp.sum(weights, axis=0, keepdims=True)
+            lse_ref[0, pl.ds(head, 1), rows] = top + jnp.log(total)
+            probs = (weights * (1.0 / total)).astype(jnp.bfloat16)
+            parts.append(
+                jnp.dot(
+                    flipped[head * size : (head + 1) * size, :upto],
+                    probs,
+                    preferred_element_type=jnp.float32,
+                )
+            )
+        mixed_ref[0, rows, :] = jnp.concatenate(parts, axis=0).T
+
+
+def attend(queries, keys, values, segs, size, name):
+    count, length, width = queries.shape
+    heads = width // size
+    whole = pl.BlockSpec((1, length, width), lambda i: (i, 0, 0))
+    return pl.pallas_call(
+        functools.partial(attend_kernel, size, min(256, length)),
+        grid=(count,),
+        out_shape=(
+            jax.ShapeDtypeStruct((count, length, width), jnp.float32),
+            jax.ShapeDtypeStruct((count, heads, length), jnp.float32),
+        ),
+        in_specs=[
+            whole,
+            whole,
+            whole,
+            pl.BlockSpec((1, length, 1), lambda i: (i, 0, 0)),
+            pl.BlockSpec((1, 1, length), lambda i: (i, 0, 0)),
+        ],
+        out_specs=(whole, pl.BlockSpec((1, heads, length), lambda i: (i, 0, 0))),
+        compiler_params=pltpu.CompilerParams(vmem_limit_bytes=48 << 20),
+        name=name,
+    )(queries, keys, values, segs[:, :, None], segs[:, None, :])
+
+
+def attend_back_kernel(
+    size,
+    block,
+    q_ref,
+    k_ref,
+    v_ref,
+    back_ref,
+    mixed_ref,
+    lse_ref,
+    key_seg_ref,
+    query_seg_ref,
+    q_back_ref,
+    k_back_ref,
+    v_back_ref,
+    k_sum,
+    v_sum,
+):
+    length, width = q_ref.shape[1:]
+    heads = width // size
+    scale = size**-0.5
+    flipped = k_ref[0].T
+    k_sum[...] = jnp.zeros_like(k_sum)
+    v_sum[...] = jnp.zeros_like(v_sum)
+    for first in range(0, length, block):
+        upto = first + block
+        rows = pl.ds(first, block)
+        before = pl.ds(0, upto)
+        allowed = used_pairs(
+            key_seg_ref[0, before, :], query_seg_ref[0, :, rows], first, upto, block
+        )
+        keys = k_ref[0, before, :]
+        values = v_ref[0, before, :]
+        query = q_ref[0, rows, :] * jnp.asarray(scale, jnp.bfloat16)
+        back = back_ref[0, rows, :]
+        product = (back.astype(jnp.float32) * mixed_ref[0, rows, :]).T
+        parts = []
+        for head in range(heads):
+            lanes = head_lanes(width, head, size)
+            own = jnp.where(lanes, query, jnp.zeros_like(query))
+            own_back = jnp.where(lanes, back, jnp.zeros_like(back))
+            delta = jnp.sum(product[head * size : (head + 1) * size, :], axis=0, keepdims=True)
+            scores = across(keys, own) - lse_ref[0, pl.ds(head, 1), rows]
+            probs = jnp.where(allowed, jnp.exp(jnp.where(allowed, scores, 0.0)), 0.0)
+            score_back = (probs * (across(values, own_back) - delta)).astype(jnp.bfloat16)
+            v_sum[before, :] += jnp.dot(
+                probs.astype(jnp.bfloat16), own_back, preferred_element_type=jnp.float32
+            )
+            k_sum[before, :] += jnp.dot(score_back, own, preferred_element_type=jnp.float32)
+            parts.append(
+                jnp.dot(
+                    flipped[head * size : (head + 1) * size, :upto],
+                    score_back,
+                    preferred_element_type=jnp.float32,
+                )
+            )
+        q_back_ref[0, rows, :] = (jnp.concatenate(parts, axis=0).T * scale).astype(jnp.bfloat16)
+    k_back_ref[0] = k_sum[...].astype(jnp.bfloat16)
+    v_back_ref[0] = v_sum[...].astype(jnp.bfloat16)
+
+
+def attend_back(queries, keys, values, back, mixed, lse, segs, size, name):
+    count, length, width = queries.shape
+    heads = width // size
+    whole = pl.BlockSpec((1, length, width), lambda i: (i, 0, 0))
+    shape = jax.ShapeDtypeStruct((count, length, width), jnp.bfloat16)
+    return pl.pallas_call(
+        functools.partial(attend_back_kernel, size, min(256, length)),
+        grid=(count,),
+        out_shape=(shape, shape, shape),
+        in_specs=[whole] * 5
+        + [
+            pl.BlockSpec((1, heads, length), lambda i: (i, 0, 0)),
+            pl.BlockSpec((1, length, 1), lambda i: (i, 0, 0)),
+            pl.BlockSpec((1, 1, length), lambda i: (i, 0, 0)),
+        ],
+        out_specs=(whole, whole, whole),
+        scratch_shapes=[pltpu.VMEM((length, width), jnp.float32)] * 2,
+        compiler_params=pltpu.CompilerParams(vmem_limit_bytes=48 << 20),
+        name=name,
+    )(queries, keys, values, back, mixed, lse, segs[:, :, None], segs[:, None, :])
+
+
+def near_half(blocks, ns, group):
+    flip = blocks.reshape((2, ns) + blocks.shape[1:])[::-1].reshape(blocks.shape)
+    return jnp.where(group == 0, blocks, flip)
+
+
+def on_device_halves(
+    tokens,
+    segments,
+    exit_layer,
+    first_gain,
+    first_shift,
+    query_weight,
+    query_bias,
+    key_weight,
+    value_weight,
+    value_bias,
+    output_weight,
+    output_bias,
+    second_gain,
+    second_shift,
+    up_weight,
+    up_bias,
+    down_weight,
+    down_bias,
+    cotangent,
+):
+    rows, width = tokens.shape[1:]
+    nd, ns = lax.axis_size("dp"), lax.axis_size("seq")
+    ndev, ranks = nd * ns, nd * ns // 2
+    size = width // HEADS
+    hidden_size = up_weight.shape[1]
+    w = place()
+    group = w["g"]
+    me = w["z"] * ns + w["s"]
+    mirror = [(d, nd - 1 - d) for d in range(nd)]
+
+    def trade(value):
+        return lax.ppermute(value, "dp", mirror)
+
+    def pair(own, other):
+        return jnp.where(group == 0, own, other), jnp.where(group == 0, other, own)
+
+    def pieces(weight):
+        cut = weight.reshape(weight.shape[0], 2, 2, ns, -1)
+        low, high = cut[:, 0], cut[:, 1, ::-1]
+        both = jnp.stack([low, high], axis=3)
+        return both.transpose(1, 2, 0, 3, 4).reshape(ranks, weight.shape[0], -1)
+
+    def whole_rows(swapped):
+        mine, other = swapped, trade(swapped)
+        low, high = pair(mine, other)
+        flat = high.reshape((2, ns) + high.shape[1:])[::-1]
+        return jnp.concatenate([low.reshape(-1, low.shape[-1]), flat.reshape(-1, low.shape[-1])])
+
+    def own_rows(gradient):
+        half = gradient.shape[0] // 2
+        low, high = gradient[:half], gradient[half:]
+        sent = jnp.where(group == 0, high, low).astype(jnp.bfloat16)
+        kept = jnp.where(group == 0, low, high)
+        total = (kept + trade(sent).astype(jnp.float32)).astype(jnp.bfloat16)
+        return near_half(total.reshape(ranks, -1, total.shape[-1]), ns, group)
+
+    def from_pieces(blocks, take):
+        cut = blocks.reshape(2, ns, blocks.shape[1], 2, take)
+        low, high = cut[:, :, :, 0], cut[::-1, :, :, 1]
+        both = jnp.stack([low, high]).transpose(3, 0, 1, 2, 4)
+        return both.reshape(blocks.shape[1], -1).astype(jnp.float32)
+
+    def own_block(gradient):
+        half = gradient.shape[0] // 2
+        low, high = gradient[:half], gradient[half:]
+        sent = jnp.where(group == 0, high, low).astype(jnp.bfloat16)
+        return jnp.where(group == 0, low, high) + trade(sent).astype(jnp.float32)
+
+    vector_parts = [
+        first_gain,
+        first_shift,
+        query_bias,
+        value_bias,
+        output_bias,
+        second_gain,
+        second_shift,
+        down_bias,
+        up_bias,
+    ]
+    vectors = lax.all_gather(jnp.concatenate(vector_parts), ("dp", "seq"), axis=0)
+    cuts, at = [], 0
+    for part in vector_parts:
+        cuts.append(vectors[:, at : at + part.shape[0]])
+        at += part.shape[0]
+    full = [cut.reshape(-1).astype(jnp.float32) for cut in cuts]
+    gain_one, shift_one, _, _, output_shift, gain_two, shift_two, down_shift, _ = full
+    low_at = me
+    high_at = (nd - 1 - w["z"]) * ns + w["s"]
+
+    def rank_vector(cut):
+        return jnp.concatenate(
+            [
+                lax.dynamic_index_in_dim(cut, low_at, 0, keepdims=False),
+                lax.dynamic_index_in_dim(cut, high_at, 0, keepdims=False),
+            ]
+        ).astype(jnp.float32)
+
+    query_shift, value_shift, up_shift = (rank_vector(cuts[i]) for i in (2, 3, 8))
+    attend_pieces = jnp.concatenate(
+        [pieces(query_weight), pieces(key_weight), pieces(value_weight)], axis=2
+    )
+    attend_weight = whole_rows(group_swap(attend_pieces, "swap_attend", 0))
+    output_rows = jnp.concatenate(pair(output_weight, trade(output_weight)))
+    up_columns = whole_rows(group_swap(pieces(up_weight), "swap_up", 1))
+    down_rows = jnp.concatenate(pair(down_weight, trade(down_weight)))
+
+    beside_dp = [(d, d + 1 - 2 * (d % 2)) for d in range(nd)]
+    other_segs = lax.ppermute(segments, "dp", beside_dp)
+    segs = jnp.concatenate(
+        [
+            jnp.where(w["z"] == 0, segments, other_segs),
+            jnp.where(w["z"] == 0, other_segs, segments),
+        ]
+    )
+
+    keep = (exit_layer > LAYER).astype(jnp.float32).reshape(rows, 1)
+    inputs = tokens.astype(jnp.float32).reshape(rows, width)
+    upstream = cotangent.astype(jnp.float32).reshape(rows, width)
+    branch_back_own = (keep * upstream).astype(jnp.bfloat16)
+
+    def gathered(own, name, cid):
+        return cube_gather(own, name, cid).reshape(-1, own.shape[1])
+
+    def scattered(partial, name, cid):
+        return cube_scatter(partial.reshape(2, 2, 2, 2, rows, -1), name, cid)
+
+    normed_one = gathered(
+        layer_norm(inputs, gain_one, shift_one).astype(jnp.bfloat16), "gather_one", 2
+    )
+    pre = jnp.dot(normed_one, attend_weight, preferred_element_type=jnp.float32)
+    take = 2 * size
+    queries = (pre[:, :take] + query_shift).astype(jnp.bfloat16).reshape(2, -1, take)
+    keys = pre[:, take : 2 * take].astype(jnp.bfloat16).reshape(2, -1, take)
+    values = (pre[:, 2 * take :] + value_shift).astype(jnp.bfloat16).reshape(2, -1, take)
+    mixed_full, lse = attend(queries, keys, values, segs, size, "attend")
+    mixed = mixed_full.reshape(-1, take).astype(jnp.bfloat16)
+    attention = scattered(
+        jnp.dot(mixed, output_rows, preferred_element_type=jnp.float32).astype(jnp.bfloat16),
+        "scatter_attention",
+        3,
+    )
+    middle = inputs + keep * (attention + output_shift)
+    normed_two = gathered(
+        layer_norm(middle, gain_two, shift_two).astype(jnp.bfloat16), "gather_two", 4
+    )
+    branch_back = gathered(branch_back_own, "gather_branch_back", 5)
+    before = jnp.dot(normed_two, up_columns, preferred_element_type=jnp.float32) + up_shift
+    active, pull_active = jax.vjp(activate, before)
+    hidden = active.astype(jnp.bfloat16)
+    hidden_back = transposed(branch_back, down_rows)
+    pre_back = pull_active(hidden_back)[0].astype(jnp.bfloat16)
+    normed_two_back = scattered(
+        transposed(pre_back, up_columns).astype(jnp.bfloat16), "scatter_normed_two_back", 6
+    )
+    down_gradient = own_block(leading(hidden, branch_back))
+    up_gradient = own_rows(leading(normed_two, pre_back))
+    norm_result, pull_two = jax.vjp(layer_norm, middle, gain_two, shift_two)
+    middle_part, gain_two_sum, shift_two_sum = pull_two(normed_two_back)
+    middle_back = upstream + middle_part
+    attention_back_own = (keep * middle_back).astype(jnp.bfloat16)
+    attention_back = gathered(attention_back_own, "gather_attention_back", 7)
+    mixed_back = transposed(attention_back, output_rows).astype(jnp.bfloat16)
+    queries_back, keys_back, values_back = attend_back(
+        queries, keys, values, mixed_back.reshape(2, -1, take), mixed_full, lse, segs, size, "attend_back"
+    )
+    stacked = jnp.concatenate([queries_back, keys_back, values_back], axis=2).reshape(-1, 3 * take)
+    normed_one_back = scattered(
+        transposed(stacked, attend_weight).astype(jnp.bfloat16), "scatter_normed_one_back", 8
+    )
+    branch = scattered(
+        jnp.dot(hidden, down_rows, preferred_element_type=jnp.float32).astype(jnp.bfloat16),
+        "scatter_branch",
+        9,
+    )
+    layer_out = (middle + keep * (branch + down_shift)).astype(jnp.bfloat16)
+    output_gradient = own_block(leading(mixed, attention_back))
+    attend_gradient = own_rows(leading(normed_one, stacked))
+    norm_first, pull_one = jax.vjp(layer_norm, inputs, gain_one, shift_one)
+    inputs_part, gain_one_sum, shift_one_sum = pull_one(normed_one_back)
+    tokens_gradient = (middle_back + inputs_part).astype(jnp.bfloat16)
+
+    up_rows = from_pieces(group_swap(up_gradient, "swap_up_gradient", 10), hidden_size // ndev)
+    attend_rows = group_swap(attend_gradient, "swap_attend_gradient", 11)
+    matrix_rows = [
+        from_pieces(attend_rows[:, :, i * take : (i + 1) * take], size) for i in range(3)
+    ]
+
+    def summed(value):
+        return jnp.sum(value.astype(jnp.float32), axis=0)
+
+    own_sums = [
+        gain_one_sum,
+        shift_one_sum,
+        gain_two_sum,
+        shift_two_sum,
+        summed(attention_back_own),
+        summed(branch_back_own),
+    ]
+    share = width // ndev
+    dense = jnp.concatenate([value.reshape(ndev, share) for value in own_sums], axis=1)
+    rank_sums = jnp.concatenate(
+        [
+            summed(queries_back.reshape(-1, take)).reshape(2, -1),
+            summed(values_back.reshape(-1, take)).reshape(2, -1),
+            summed(pre_back).reshape(2, -1),
+        ],
+        axis=1,
+    )
+    number = jnp.arange(ndev)[:, None]
+    sparse = jnp.where(
+        number == low_at, rank_sums[0], jnp.where(number == high_at, rank_sums[1], 0.0)
+    )
+    letter = jnp.concatenate([dense, sparse], axis=1)
+    letter = jnp.pad(letter, ((0, 0), (0, -letter.shape[1] % 1024))).reshape(ndev, -1, 128)
+    mail = jnp.sum(world_swap(letter, "swap_vectors", 12), axis=0).reshape(-1)
+    vector_out, at = [], 0
+    for part in (share,) * 6 + (size, size, hidden_size // ndev):
+        vector_out.append(mail[at : at + part])
+        at += part
+    (
+        gain_one_part,
+        shift_one_part,
+        gain_two_part,
+        shift_two_part,
+        output_shift_part,
+        down_shift_part,
+        query_shift_part,
+        value_shift_part,
+        up_shift_part,
+    ) = vector_out
+    return (
+        layer_out.reshape(tokens.shape),
+        tokens_gradient.reshape(tokens.shape),
+        gain_one_part,
+        shift_one_part,
+        matrix_rows[0],
+        query_shift_part,
+        matrix_rows[1],
+        matrix_rows[2],
+        value_shift_part,
+        output_gradient,
+        output_shift_part,
+        gain_two_part,
+        shift_two_part,
+        up_rows,
+        up_shift_part,
+        down_gradient,
+        down_shift_part,
+    )
+
+
 def solution(mesh):
     placed = (
         P("dp", "seq", None),
@@ -389,8 +1017,9 @@
         P(("dp", "seq")),
         P("dp", "seq", None),
     )
+    halves = mesh.shape["dp"] == 4 and mesh.shape["seq"] == 8
     return jax.shard_map(
-        on_device,
+        on_device_halves if halves else on_device,
         mesh=mesh,
         in_specs=placed,
         out_specs=(

time: 3820 us -> 811 us (0.21)
  waiting for transfers between devices: 3170 us -> 0.02 us
  Pallas kernels: 0 us -> 530 us
  matrix products: 307 us -> 81.1 us
  other arithmetic: 109 us -> 39.3 us
  local copies, waits for them, and re-layouts: 99.3 us -> 53.4 us
    unnamed x15 -> x0, waiting for transfers between devices: 1870 us -> none
    reduce_scatter x1 -> x0, waiting for transfers between devices: 698 us -> none  [on_device(): lax.psum_scatter(leading(hidden, branch_back), ('dp', 'seq'), scatter_dim...]
    all_gather x10 -> x0, waiting for transfers between devices: 606 us -> none  [the longest x1 191 us: on_device(): lax.all_gather(up_weight, ('dp', 'seq'), axis=0, tiled=True)]
    pallas_call x0 -> x15, Pallas kernels: none -> 530 us  [the longest x4 204 us: cube_scatter(): pl.pallas_call(scatter_kernel, out_shape=jax.ShapeDtypeStruct((rows, widt...]
    dot_general x62 -> x4, matrix products: 164 us -> 25.2 us  [the longest x1 8.05 us: on_device_halves(): jnp.dot(hidden, down_rows, preferred_element_type=jnp.float32)]
    concatenate x2 -> x4, other arithmetic: 88.1 us -> 1.28 us  [the longest x1 0.99 us: on_device_halves(): jnp.concatenate([pieces(query_weight), pieces(key_weight), pieces(value_w...]
    dot_general x4, matrix products: 77.8 us -> 27.7 us  [leading(): lax.dot_general(left, right, (((0,), (0,)), ((), ())), preferred_element_...]
    unnamed x1 -> x0, blocking collectives: 43 us -> none
  transfers between devices with their start and end apart: 13 -> 9, of which waited for: 10 -> 0; matrix products, arithmetic and copies ran while one was open for 10% -> 11% of each run, Pallas kernels for 0% -> 49%
where the time goes in v1:
time: 811 us; the launch traced here: 803 us
  Pallas kernels  530 us (65%)
  matrix products  81.1 us (10%)
  blocking collectives  80.5 us (10%)
  local copies, waits for them, and re-layouts  53.4 us (7%)
  other arithmetic  39.3 us (5%)
  starting transfers between devices  16.1 us (2%)
    pallas_call x4, Pallas kernels, cube_scatter(): pl.pallas_call(scatter_kernel, out_shape=jax.ShapeDtypeStruct((rows, widt...  204 us
    pallas_call x4, Pallas kernels, cube_gather(): pl.pallas_call(gather_kernel, out_shape=jax.ShapeDtypeStruct((2, 2, 2, 2,...  197 us
    pallas_call x5, Pallas kernels, swap(): pl.pallas_call(functools.partial(swap_kernel, device_of, row), out_shape=...  111 us
    all_gather x1, blocking collectives, on_device_halves(): lax.all_gather(jnp.concatenate(vector_parts), ('dp', 'seq'), axis=0)  80.5 us
    dot_general x4, matrix products, transposed(): lax.dot_general(left, right, (((1,), (1,)), ((), ())), preferred_element_...  28.1 us
    dot_general x4, matrix products, leading(): lax.dot_general(left, right, (((0,), (0,)), ((), ())), preferred_element_...  27.7 us
    unnamed x144, local copies, waits for them, and re-layouts  23 us
  transfers between devices with their start and end apart: 9, of which 0 were waited for; matrix products, arithmetic and copies ran while one was open for 11% of the time, Pallas kernels for 49%

profile of v1, /device:TPU:0, one launch (start us, length us, event | category | flops | bytes accessed | tf_op | source)
XLA Modules:
  0.0 803.0 jit_solution(2655376939485812389)
XLA Ops:
  0.7 1.5 reshape.376
  7.4 14.6 %swap_attend.1 = bf16[16,64,384]{2,1,0:T(8,128)(2,1)} custom-call(bf16[16,64,384]{2,1,0:T(8,128)(2,1)} %pad_maximum_fusion.12.src), custom_call_target="tpu_custom_call" | custom-call | tf_op jit(solution)/shard_map/swap_attend/pallas_call | solution.py:575
  22.0 3.6 collective-permute-start
  29.7 30.2 %swap_up.1 = bf16[16,64,512]{2,1,0:T(8,128)(2,1)} custom-call(bf16[16,64,512]{2,1,0:T(8,128)(2,1)} %reshape.391.src), custom_call_target="tpu_custom_call" | custom-call | tf_op jit(solution)/shard_map/swap_up/pallas_call | solution.py:575
  59.9 3.2 collective-permute-start.3
  64.0 80.5 %all-gather.1 = bf16[32,1,768]{2,1,0:T(2,128)(2,1)S(1)} all-gather(bf16[1,1,768]{2,1,0:T(2,128)(2,1)S(1)} %reshape.439), channel_id=2, replica_groups=mesh['dp'=4,'seq'=8] {'dp','seq'}, dimensions={0}, use_global_device_ids=true | all-gather | bytes 50688 | tf_op jit(solution)/shard_map/all_gather | solution.py:826
  146.8 83.0 %gather_one.1 = bf16[2,2,2,2,128,2048]{5,4,3,2,1,0:T(8,128)(2,1)S(1)} custom-call(bf16[128,2048]{1,0:T(8,128)(2,1)S(1)} %fusion.18.src), custom_call_target="tpu_custom_call" | custom-call | tf_op jit(solution)/shard_map/gather_one/pallas_call | solution.py:445
  229.9 3.3 copy-done.2
  234.6 2.2 broadcast_select_fusion.5
  237.8 7.1 fusion.25
  245.1 9.5 %attend.1 = (f32[2,1024,128]{2,1,0:T(8,128)S(1)}, f32[2,2,1024]{2,1,0:T(2,128)S(1)}) custom-call(bf16[2,1024,128]{2,1,0:T(8,128)(2,1)S(1)} %bitcast.194, bf16[2,1024,128]{2,1,0:T(8,128)(2,1)S(1)} %bitcast.190, bf16[2,1024,128]{2,1,0:T(8,128)(2,1)S(1)} %bitcast.192, s32[2,1024,1]{2,1,0:T(8,128)S(1)} %copy.107.key_seg_ref, ...), custom_call_target="tpu_custom_call" | custom-call | tf_op jit(solution)/shard_map/attend/pallas_call | solution.py:639
  254.7 2.3 convolution_convert_fusion.3
  257.1 38.8 %scatter_attention.1 = f32[128,2048]{1,0:T(8,128)S(1)} custom-call(bf16[2,2,2,2,128,2048]{5,4,3,2,1,0:T(8,128)(2,1)S(1)} %bitcast.176), custom_call_target="tpu_custom_call" | custom-call | tf_op jit(solution)/shard_map/scatter_attention/pallas_call | solution.py:529
  297.6 38.8 %gather_two.1 = bf16[2,2,2,2,128,2048]{5,4,3,2,1,0:T(8,128)(2,1)S(1)} custom-call(bf16[128,2048]{1,0:T(8,128)(2,1)S(1)} %add_convert_fusion.4.src), custom_call_target="tpu_custom_call" | custom-call | tf_op jit(solution)/shard_map/gather_two/pallas_call | solution.py:445
  336.3 3.2 copy-done.3
  339.6 38.8 %gather_branch_back.1 = bf16[2,2,2,2,128,2048]{5,4,3,2,1,0:T(8,128)(2,1)S(1)} custom-call(bf16[128,2048]{1,0:T(8,128)(2,1)S(1)} %get-tuple-element.39.src), custom_call_target="tpu_custom_call" | custom-call | tf_op jit(solution)/shard_map/gather_branch_back/pallas_call | solution.py:445
  378.4 3.3 copy-done.4
  381.7 3.0 broadcast_select_fusion.3
  384.7 2.3 rev.41
  387.0 7.8 fusion.8
  394.8 11.5 %fusion.47 = f32[512,2048]{1,0:T(8,128)} fusion(bf16[2048,2048]{1,0:T(8,128)(2,1)} %bitcast.186, f32[2048,512]{1,0:T(8,128)S(1)} %fusion.8, f32[512]{0:T(512)S(1)} %maximum_convert_fusion), kind=kOutput, calls=%fused_computation.160 | convolution fusion | flops 4305453056 | bytes 16779264 | tf_op jit(solution)/shard_map/dot_general | solution.py:37
  406.3 1.8 broadcast_select_fusion.1
  408.2 9.9 %convert_reduce_fusion = (f32[512]{0:T(512)}, bf16[2048,512]{1,0:T(8,128)(2,1)}) fusion(f32[2048,512]{1,0:T(8,128)S(1)} %fusion.8, f32[512]{0:T(512)S(1)} %maximum_convert_fusion, bf16[2048,2048]{1,0:T(8,128)(2,1)S(1)} %bitcast.189, bf16[256,2048]{1,0:T(8,128)(2,1)S(1)} %get-tuple-element.51, bf16[256,2048]{1,0:T(8,128)(2,1)S(1)} %get-tuple-element.50), kind=kOutput, calls=%fused_computation.13 | convolution fusion | flops 4323278336 | bytes 16781312 | tf_op jit(solution)/shard_map/dot_general | solution.py:31
  418.1 7.9 fusion.61
  426.0 8.0 %convolution_convert_fusion.1 = bf16[2048,2048]{1,0:T(8,128)(2,1)} fusion(bf16[2048,512]{1,0:T(8,128)(2,1)S(1)} %copy-done.60, bf16[1024,512]{1,0:T(8,128)(2,1)S(1)} %bitcast.215, bf16[1024,512]{1,0:T(8,128)(2,1)S(1)} %bitcast.212), kind=kOutput, calls=%fused_computation.1 | convolution fusion | flops 4303355904 | bytes 12582912 | tf_op jit(solution)/shard_map/dot_general | solution.py:31
  434.0 8.1 %convolution_convert_fusion.2 = bf16[2048,2048]{1,0:T(8,128)(2,1)S(1)} fusion(bf16[256,2048]{1,0:T(8,128)(2,1)S(1)} %get-tuple-element.51, bf16[256,2048]{1,0:T(8,128)(2,1)S(1)} %get-tuple-element.50, f32[2048,512]{1,0:T(8,128)} %copy-done.59, f32[512]{0:T(512)S(1)} %maximum_convert_fusion), kind=kOutput, calls=%fused_computation.2 | convolution fusion | flops 4313841664 | bytes 14682112 | tf_op jit(solution)/shard_map/dot_general | solution.py:917
  442.1 3.4 copy-done.1
  445.5 39.4 %scatter_normed_two_back.1 = f32[128,2048]{1,0:T(8,128)S(1)} custom-call(bf16[2,2,2,2,128,2048]{5,4,3,2,1,0:T(8,128)(2,1)S(1)} %bitcast.179), custom_call_target="tpu_custom_call" | custom-call | tf_op jit(solution)/shard_map/scatter_normed_two_back/pallas_call | solution.py:529
  485.8 39.3 %scatter_branch.1 = f32[128,2048]{1,0:T(8,128)S(1)} custom-call(bf16[2,2,2,2,128,2048]{5,4,3,2,1,0:T(8,128)(2,1)S(1)} %bitcast.178), custom_call_target="tpu_custom_call" | custom-call | tf_op jit(solution)/shard_map/scatter_branch/pallas_call | solution.py:529
  527.4 36.9 %gather_attention_back.1 = bf16[2,2,2,2,128,2048]{5,4,3,2,1,0:T(8,128)(2,1)S(1)} custom-call(bf16[128,2048]{1,0:T(8,128)(2,1)S(1)} %get-tuple-element.41.src), custom_call_target="tpu_custom_call" | custom-call | tf_op jit(solution)/shard_map/gather_attention_back/pallas_call | solution.py:445
  565.6 2.4 convolution_convert_fusion.4
  568.0 7.9 attend_back.1
  576.7 7.1 fusion.59
  583.8 7.8 convolution_convert_fusion
  592.8 2.8 collective-permute-start.8
  598.6 2.8 collective-permute-start.6
  603.8 3.4 copy-done
  607.2 86.7 %scatter_normed_one_back.1 = f32[128,2048]{1,0:T(8,128)S(1)} custom-call(bf16[2,2,2,2,128,2048]{5,4,3,2,1,0:T(8,128)(2,1)S(1)} %bitcast.177), custom_call_target="tpu_custom_call" | custom-call | tf_op jit(solution)/shard_map/scatter_normed_one_back/pallas_call | solution.py:529
  700.6 34.2 %swap_vectors.1 = f32[32,8,128]{2,1,0:T(8,128)} custom-call(f32[32,8,128]{2,1,0:T(8,128)} %bitcast.223), custom_call_target="tpu_custom_call" | custom-call | tf_op jit(solution)/shard_map/swap_vectors/pallas_call | solution.py:575
  735.4 2.0 fusion.27
  739.6 2.1 convert_add_fusion.2
  741.7 2.3 add_convert_fusion.1
  745.1 13.2 %swap_attend_gradient.1 = bf16[16,64,384]{2,1,0:T(8,128)(2,1)} custom-call(bf16[16,64,384]{2,1,0:T(8,128)(2,1)} %bitcast_select_fusion.1.src), custom_call_target="tpu_custom_call" | custom-call | tf_op jit(solution)/shard_map/swap_attend_gradient/pallas_call | solution.py:575
  769.8 3.2 add_convert_fusion
  774.2 19.1 %swap_up_gradient.1 = bf16[16,64,512]{2,1,0:T(8,128)(2,1)} custom-call(bf16[16,64,512]{2,1,0:T(8,128)(2,1)} %bitcast_select_fusion.src), custom_call_target="tpu_custom_call" | custom-call | tf_op jit(solution)/shard_map/swap_up_gradient/pallas_call | solution.py:575
  794.7 1.9 fusion.53
  797.0 1.5 copy.133
  799.8 3.0 convert_add_fusion
  (271 shorter events, 54.1 us)
Async XLA Ops:
  4.8 20.8 %copy-start.41 = (s32[1,1024]{1,0:T(1,128)S(1)}, s32[1,1024]{1,0:T(1,128)}, u32[]{:S(2)}) copy-start(s32[1,1024]{1,0:T(1,128)} %param.20) | copy-start | bytes 12292
  4.8 20.8 %copy-start.33 = (bf16[64,2048]{1,0:T(8,128)(2,1)S(1)}, bf16[64,2048]{1,0:T(8,128)(2,1)}, u32[]{:S(2)}) copy-start(bf16[64,2048]{1,0:T(8,128)(2,1)} %param.29) | copy-start | bytes 786436
  4.8 21.7 %copy-start.24 = (bf16[64,8192]{1,0:T(8,128)(2,1)S(1)}, bf16[64,8192]{1,0:T(8,128)(2,1)}, u32[]{:S(2)}) copy-start(bf16[64,8192]{1,0:T(8,128)(2,1)} %param.33) | copy-start | bytes 3145732
  22.0 212.6 %collective-permute-start = (bf16[16,64,384]{2,1,0:T(8,128)(2,1)}, bf16[16,64,384]{2,1,0:T(8,128)(2,1)}, u32[]{:S(2)}, u32[]{:S(2)}) collective-permute-start(bf16[16,64,384]{2,1,0:T(8,128)(2,1)} %swap_attend.1), channel_id=1, source_target_pairs={{0,24},{8,16},{16,8},{24,0},{1,25},{9,17},{17,9},{25,1},{2,26},{10... | collective-permute-start | bytes 2359304 | tf_op jit(solution)/shard_map/ppermute | solution.py:778
  25.6 207.8 %collective-permute-start.1 = (s32[1,1024]{1,0:T(1,128)S(1)}, s32[1,1024]{1,0:T(1,128)S(1)}, u32[]{:S(2)}, u32[]{:S(2)}) collective-permute-start(s32[1,1024]{1,0:T(1,128)S(1)} %copy-done.41), channel_id=1, source_target_pairs={{0,8},{8,0},{16,24},{24,16},{1,9},{9,1},{17,25},{25,17},{2,10},{10... | collective-permute-start | bytes 12296 | tf_op jit(solution)/shard_map/ppermute | solution.py:854
  25.6 208.2 %collective-permute-start.2 = (bf16[64,2048]{1,0:T(8,128)(2,1)S(1)}, bf16[64,2048]{1,0:T(8,128)(2,1)S(1)}, u32[]{:S(2)}, u32[]{:S(2)}) collective-permute-start(bf16[64,2048]{1,0:T(8,128)(2,1)S(1)} %copy-done.33), channel_id=1, source_target_pairs={{0,24},{8,16},{16,8},{24,0},{1,25},{9,17},{17,9},{25,1},{2,26},{10... | collective-permute-start | bytes 786440 | tf_op jit(solution)/shard_map/ppermute | solution.py:778
  26.9 36.9 %copy-start.47 = (bf16[64]{0:T(256)(128)(2,1)S(1)}, bf16[64]{0:T(256)(128)(2,1)}, u32[]{:S(2)}) copy-start(bf16[64]{0:T(256)(128)(2,1)} %param.22) | copy-start | bytes 388
  26.9 36.9 %copy-start.48 = (bf16[64]{0:T(256)(128)(2,1)S(1)}, bf16[64]{0:T(256)(128)(2,1)}, u32[]{:S(2)}) copy-start(bf16[64]{0:T(256)(128)(2,1)} %param.23) | copy-start | bytes 388
  27.0 36.9 %copy-start.49 = (bf16[64]{0:T(256)(128)(2,1)S(1)}, bf16[64]{0:T(256)(128)(2,1)}, u32[]{:S(2)}) copy-start(bf16[64]{0:T(256)(128)(2,1)} %param.25) | copy-start | bytes 388
  27.0 36.9 %copy-start.50 = (bf16[64]{0:T(256)(128)(2,1)S(1)}, bf16[64]{0:T(256)(128)(2,1)}, u32[]{:S(2)}) copy-start(bf16[64]{0:T(256)(128)(2,1)} %param.28) | copy-start | bytes 388
  27.0 36.9 %copy-start.51 = (bf16[64]{0:T(256)(128)(2,1)S(1)}, bf16[64]{0:T(256)(128)(2,1)}, u32[]{:S(2)}) copy-start(bf16[64]{0:T(256)(128)(2,1)} %param.30) | copy-start | bytes 388
  27.0 36.9 %copy-start.52 = (bf16[64]{0:T(256)(128)(2,1)S(1)}, bf16[64]{0:T(256)(128)(2,1)}, u32[]{:S(2)}) copy-start(bf16[64]{0:T(256)(128)(2,1)} %param.31) | copy-start | bytes 388
  27.0 36.9 %copy-start.53 = (bf16[64]{0:T(256)(128)(2,1)S(1)}, bf16[64]{0:T(256)(128)(2,1)}, u32[]{:S(2)}) copy-start(bf16[64]{0:T(256)(128)(2,1)} %param.32) | copy-start | bytes 388
  27.0 36.9 %copy-start.54 = (bf16[64]{0:T(256)(128)(2,1)S(1)}, bf16[64]{0:T(256)(128)(2,1)}, u32[]{:S(2)}) copy-start(bf16[64]{0:T(256)(128)(2,1)} %param.36) | copy-start | bytes 388
  27.0 36.8 %copy-start.55 = (bf16[256]{0:T(256)(128)(2,1)S(1)}, bf16[256]{0:T(256)(128)(2,1)}, u32[]{:S(2)}) copy-start(bf16[256]{0:T(256)(128)(2,1)} %param.34) | copy-start | bytes 1540
  27.0 118.2 %copy-start.9 = (bf16[1,128,2048]{2,1,0:T(8,128)(2,1)S(1)}, bf16[1,128,2048]{2,1,0:T(8,128)(2,1)}, u32[]{:S(2)}) copy-start(bf16[1,128,2048]{2,1,0:T(8,128)(2,1)} %param.19) | copy-start | bytes 1572868
  27.2 119.0 %copy-start.58 = (s32[1,128]{1,0:T(1,128)S(1)}, s32[1,128]{1,0:T(1,128)}, u32[]{:S(2)}) copy-start(s32[1,128]{1,0:T(1,128)} %param.21) | copy-start | bytes 1540
  59.9 321.8 %collective-permute-start.3 = (bf16[16,64,512]{2,1,0:T(8,128)(2,1)}, bf16[16,64,512]{2,1,0:T(8,128)(2,1)}, u32[]{:S(2)}, u32[]{:S(2)}) collective-permute-start(bf16[16,64,512]{2,1,0:T(8,128)(2,1)} %swap_up.1), channel_id=1, source_target_pairs={{0,24},{8,16},{16,8},{24,0},{1,25},{9,17},{17,9},{25,1},{2,26},{10... | collective-permute-start | bytes 3145736 | tf_op jit(solution)/shard_map/ppermute | solution.py:778
  63.2 343.1 %collective-permute-start.4 = (bf16[256,2048]{1,0:T(8,128)(2,1)}, bf16[256,2048]{1,0:T(8,128)(2,1)}, u32[]{:S(2)}, u32[]{:S(2)}) collective-permute-start(bf16[256,2048]{1,0:T(8,128)(2,1)} %param.35), channel_id=1, source_target_pairs={{0,24},{8,16},{16,8},{24,0},{1,25},{9,17},{17,9},{25,1},{2,26},{10... | collective-permute-start | bytes 3145736 | tf_op jit(solution)/shard_map/ppermute | solution.py:778
  145.4 84.5 %copy-start.37 = (f32[128]{0:T(128)}, f32[128]{0:T(128)S(1)}, u32[]{:S(2)}) copy-start(f32[128]{0:T(128)S(1)} %broadcast_multiply_fusion.1) | copy-start | bytes 1540
  146.2 83.7 %copy-start.39 = (f32[128]{0:T(128)}, f32[128]{0:T(128)S(1)}, u32[]{:S(2)}) copy-start(f32[128]{0:T(128)S(1)} %fusion.35) | copy-start | bytes 1540
  146.8 87.8 %copy-start.22 = (bf16[16,64,384]{2,1,0:T(8,128)(2,1)S(1)}, bf16[16,64,384]{2,1,0:T(8,128)(2,1)}, u32[]{:S(2)}) copy-start(bf16[16,64,384]{2,1,0:T(8,128)(2,1)} %swap_attend.1) | copy-start | bytes 2359300
  257.1 38.8 %copy-start.19 = (bf16[1,128,2048]{2,1,0:T(8,128)(2,1)S(1)}, bf16[1,128,2048]{2,1,0:T(8,128)(2,1)}, u32[]{:S(2)}) copy-start(bf16[1,128,2048]{2,1,0:T(8,128)(2,1)} %param.37) | copy-start | bytes 1572868
  387.0 21.1 %slice-start.2 = ((s8[8388608]{0:T(1024)(128)(4,1)}), s8[4194304]{0:T(1024)(128)(4,1)S(1)}, s32[]{:S(2)}) async-start(s8[8388608]{0:T(1024)(128)(4,1)} %bitcast.187), calls=%async_computation.2 | async-start | bytes 8388608
  394.8 13.3 %copy-start.59 = (f32[2048,512]{1,0:T(8,128)}, f32[2048,512]{1,0:T(8,128)S(1)}, u32[]{:S(2)}) copy-start(f32[2048,512]{1,0:T(8,128)S(1)} %fusion.8) | copy-start | bytes 12582916
  394.8 13.4 %slice-start.3 = ((s8[8388608]{0:T(1024)(128)(4,1)}), s8[4194304]{0:T(1024)(128)(4,1)S(1)}, s32[]{:S(2)}) async-start(s8[8388608]{0:T(1024)(128)(4,1)} %bitcast.187), calls=%async_computation.3 | async-start | bytes 8388608
  445.5 39.4 %copy-start.8 = (f32[128,2048]{1,0:T(8,128)S(1)}, f32[128,2048]{1,0:T(8,128)}, u32[]{:S(2)}) copy-start(f32[128,2048]{1,0:T(8,128)} %copy-done.7) | copy-start | bytes 3145732
  526.4 37.8 %copy-start.13 = (f32[128,2048]{1,0:T(8,128)}, f32[128,2048]{1,0:T(8,128)S(1)}, u32[]{:S(2)}) copy-start(f32[128,2048]{1,0:T(8,128)S(1)} %get-tuple-element.43) | copy-start | bytes 3145732
  526.4 37.8 %copy-start.46 = (f32[128]{0:T(128)}, f32[128]{0:T(128)S(1)}, u32[]{:S(2)}) copy-start(f32[128]{0:T(128)S(1)} %negate_multiply_fusion.1) | copy-start | bytes 1540
  527.4 36.9 %copy-start.16 = (bf16[2,1024,128]{2,1,0:T(8,128)(2,1)S(1)}, bf16[2,1024,128]{2,1,0:T(8,128)(2,1)}, u32[]{:S(2)}) copy-start(bf16[2,1024,128]{2,1,0:T(8,128)(2,1)} %copy-done.15) | copy-start | bytes 1572868
  565.6 32.3 %copy-start.18 = (f32[128,2048]{1,0:T(8,128)}, f32[128,2048]{1,0:T(8,128)S(1)}, u32[]{:S(2)}) copy-start(f32[128,2048]{1,0:T(8,128)S(1)} %fusion.60) | copy-start | bytes 3145732
  583.8 17.6 %copy-start.17 = (f32[2048,384]{1,0:T(8,128)}, f32[2048,384]{1,0:T(8,128)S(1)}, u32[]{:S(2)}) copy-start(f32[2048,384]{1,0:T(8,128)S(1)} %fusion.59) | copy-start | bytes 9437188
  583.8 11.8 %copy-start.10 = (f32[2048,512]{1,0:T(8,128)S(1)}, f32[2048,512]{1,0:T(8,128)}, u32[]{:S(2)}) copy-start(f32[2048,512]{1,0:T(8,128)} %fusion.61) | copy-start | bytes 12582916
  591.7 12.0 %copy-start.45 = (f32[512]{0:T(512)S(1)}, f32[512]{0:T(512)}, u32[]{:S(2)}) copy-start(f32[512]{0:T(512)} %get-tuple-element.102) | copy-start | bytes 6148
  592.8 205.7 %collective-permute-start.8 = (bf16[256,2048]{1,0:T(8,128)(2,1)}, bf16[256,2048]{1,0:T(8,128)(2,1)}, u32[]{:S(2)}, u32[]{:S(2)}) collective-permute-start(bf16[256,2048]{1,0:T(8,128)(2,1)} %select_convert_fusion), channel_id=1, source_target_pairs={{0,24},{8,16},{16,8},{24,0},{1,25},{9,17},{17,9},{25,1},{2,26},{10... | collective-permute-start | bytes 3145736 | tf_op jit(solution)/shard_map/ppermute | solution.py:778
  596.8 173.0 %collective-permute-start.7 = (bf16[1024,512]{1,0:T(8,128)(2,1)}, bf16[1024,512]{1,0:T(8,128)(2,1)}, u32[]{:S(2)}, u32[]{:S(2)}) collective-permute-start(bf16[1024,512]{1,0:T(8,128)(2,1)} %select_convert_fusion.1), channel_id=1, source_target_pairs={{0,24},{8,16},{16,8},{24,0},{1,25},{9,17},{17,9},{25,1},{2,26},{10... | collective-permute-start | bytes 3145736 | tf_op jit(solution)/shard_map/ppermute | solution.py:778
  598.6 141.0 %collective-permute-start.6 = (bf16[64,2048]{1,0:T(8,128)(2,1)}, bf16[64,2048]{1,0:T(8,128)(2,1)S(1)}, u32[]{:S(2)}, u32[]{:S(2)}) collective-permute-start(bf16[64,2048]{1,0:T(8,128)(2,1)} %select_convert_fusion.3), channel_id=1, source_target_pairs={{0,24},{8,16},{16,8},{24,0},{1,25},{9,17},{17,9},{25,1},{2,26},{10... | collective-permute-start | bytes 786440 | tf_op jit(solution)/shard_map/ppermute | solution.py:778
  602.5 139.1 %collective-permute-start.5 = (bf16[1024,384]{1,0:T(8,128)(2,1)}, bf16[1024,384]{1,0:T(8,128)(2,1)}, u32[]{:S(2)}, u32[]{:S(2)}) collective-permute-start(bf16[1024,384]{1,0:T(8,128)(2,1)} %select_convert_fusion.2), channel_id=1, source_target_pairs={{0,24},{8,16},{16,8},{24,0},{1,25},{9,17},{17,9},{25,1},{2,26},{10... | collective-permute-start | bytes 2359304 | tf_op jit(solution)/shard_map/ppermute | solution.py:778
  607.2 86.8 %copy-start.38 = (f32[128]{0:T(128)S(1)}, f32[128]{0:T(128)}, u32[]{:S(2)}) copy-start(f32[128]{0:T(128)} %copy-done.37) | copy-start | bytes 1540
  607.2 87.2 %copy-start.57 = (f32[128]{0:T(128)S(1)}, f32[128]{0:T(128)}, u32[]{:S(2)}) copy-start(f32[128]{0:T(128)} %copy-done.56) | copy-start | bytes 1540
  607.2 87.2 %copy-start.40 = (f32[128]{0:T(128)S(1)}, f32[128]{0:T(128)}, u32[]{:S(2)}) copy-start(f32[128]{0:T(128)} %copy-done.39) | copy-start | bytes 1540
  607.2 89.0 %copy-start.36 = (f32[2048]{0:T(1024)S(1)}, f32[2048]{0:T(1024)}, u32[]{:S(2)}) copy-start(f32[2048]{0:T(1024)} %get-tuple-element.40) | copy-start | bytes 24580
  607.2 89.7 %copy-start.35 = (f32[2048]{0:T(1024)S(1)}, f32[2048]{0:T(1024)}, u32[]{:S(2)}) copy-start(f32[2048]{0:T(1024)} %get-tuple-element.27) | copy-start | bytes 24580
  607.2 90.4 %copy-start.34 = (f32[2048]{0:T(1024)S(1)}, f32[2048]{0:T(1024)}, u32[]{:S(2)}) copy-start(f32[2048]{0:T(1024)} %get-tuple-element.31) | copy-start | bytes 24580
  607.2 91.0 %copy-start.43 = (pred[32]{0:T(512)(128)(4,1)S(1)}, pred[32]{0:T(512)(128)(4,1)}, u32[]{:S(2)}) copy-start(pred[32]{0:T(512)(128)(4,1)} %get-tuple-element.106) | copy-start | bytes 100
  607.2 91.0 %copy-start.44 = (pred[32]{0:T(512)(128)(4,1)S(1)}, pred[32]{0:T(512)(128)(4,1)}, u32[]{:S(2)}) copy-start(pred[32]{0:T(512)(128)(4,1)} %get-tuple-element.107) | copy-start | bytes 100
  694.0 41.4 %copy-start.14 = (f32[128,2048]{1,0:T(8,128)S(1)}, f32[128,2048]{1,0:T(8,128)}, u32[]{:S(2)}) copy-start(f32[128,2048]{1,0:T(8,128)} %copy-done.13) | copy-start | bytes 3145732
  694.0 41.4 %copy-start.21 = (bf16[1,128,2048]{2,1,0:T(8,128)(2,1)S(1)}, bf16[1,128,2048]{2,1,0:T(8,128)(2,1)}, u32[]{:S(2)}) copy-start(bf16[1,128,2048]{2,1,0:T(8,128)(2,1)} %param.37) | copy-start | bytes 1572868
  (26 other events, 115.0 us)

commit v2 on v1

--- a/solution.py
+++ b/solution.py
@@ -543,44 +543,92 @@
     e, s = r // n, r % n
     return (e + w["g"] * (lax.axis_size("dp") - 1 - 2 * e), s)
 
+
 def anyone(w, i):
     n = lax.axis_size("seq")
     return (i // n, i % n)
 
-def swap_kernel(device_of, row, src, out, send, recv, lsem):
+
+HALF, WORLD, SPREAD = "half", "world", "spread"
+
+
+def mail_order(w, kind, count):
+    me = w["z" if kind == HALF else "d"] * lax.axis_size("seq") + w["s"]
+    return me, [(me + k) % count for k in range(1, count)], peer if kind == HALF else anyone
+
+
+def mail_copies(w, kind, src, out, send, recv, local):
+    me, others, device_of = mail_order(w, kind, out.shape[0])
+    copies = []
+    for k, r in enumerate(others):
+        copies.append(
+            pltpu.make_async_remote_copy(
+                src_ref=src if kind == SPREAD else src.at[r],
+                dst_ref=out.at[me],
+                send_sem=send.at[k],
+                recv_sem=recv.at[k],
+                device_id=device_of(w, r),
+                device_id_type=MESH,
+            )
+        )
+    own = pltpu.make_async_copy(src if kind == SPREAD else src.at[me], out.at[me], local)
+    return copies + [own]
+
+
+def mail(w, kind, src, out, send, recv, local):
+    copies = mail_copies(w, kind, src, out, send, recv, local)
+    for cp in copies:
+        cp.start()
+    return copies
+
+
+def greet_mail(w, kinds_counts):
+    counts = dict(kinds_counts)
+    wide = max((n for kind, n in counts.items() if kind != HALF), default=0)
+    if wide:
+        _, others, device_of = mail_order(w, WORLD, wide)
+    else:
+        _, others, device_of = mail_order(w, HALF, counts[HALF])
+    greet([device_of(w, r) for r in others])
+
+
+def mail_kernel(kinds, *refs):
+    n = len(kinds)
+    srcs, outs, sems = refs[:n], refs[n : 2 * n], refs[2 * n :]
     w = place()
-    n = src.shape[0]
-    me = w[row] * lax.axis_size("seq") + w["s"]
-    others = [(me + k) % n for k in range(1, n)]
-    greet([device_of(w, r) for r in others])
-    cps = []
-    for k, r in enumerate(others):
-        cp = pltpu.make_async_remote_copy(src_ref=src.at[r], dst_ref=out.at[me], send_sem=send.at[k], recv_sem=recv.at[k], device_id=device_of(w, r), device_id_type=MESH)
-        cp.start(); cps.append(cp)
-    lc = pltpu.make_async_copy(src.at[me], out.at[me], lsem)
-    lc.start(); lc.wait()
-    for cp in cps:
+    greet_mail(w, [(kind, out.shape[0]) for kind, out in zip(kinds, outs)])
+    copies = []
+    for i, kind in enumerate(kinds):
+        copies += mail(w, kind, srcs[i], outs[i], *sems[3 * i : 3 * i + 3])
+    for cp in copies:
         cp.wait()
 
-def group_swap(blocks, name, cid):
-    return swap(peer, "z", blocks, name, cid)
-
-
-def world_swap(blocks, name, cid):
-    return swap(anyone, "d", blocks, name, cid)
-
-
-def swap(device_of, row, blocks, name, cid):
-    n = blocks.shape[0]
+
+def mail_sems(count):
+    return [
+        pltpu.SemaphoreType.DMA((count - 1,)),
+        pltpu.SemaphoreType.DMA((count - 1,)),
+        pltpu.SemaphoreType.DMA,
+    ]
+
+
+def swap(items, name, cid):
+    anywhere = pl.BlockSpec(memory_space=pl.ANY)
+    kinds = [kind for _, kind in items]
+    ndev = lax.axis_size("dp") * lax.axis_size("seq")
+    shapes = [
+        jax.ShapeDtypeStruct((ndev,) + x.shape if kind == SPREAD else x.shape, x.dtype)
+        for x, kind in items
+    ]
     return pl.pallas_call(
-        functools.partial(swap_kernel, device_of, row),
-        out_shape=jax.ShapeDtypeStruct(blocks.shape, blocks.dtype),
-        in_specs=[pl.BlockSpec(memory_space=pl.ANY)],
-        out_specs=pl.BlockSpec(memory_space=pl.ANY),
-        scratch_shapes=[pltpu.SemaphoreType.DMA((n - 1,)), pltpu.SemaphoreType.DMA((n - 1,)), pltpu.SemaphoreType.DMA],
+        functools.partial(mail_kernel, kinds),
+        out_shape=tuple(shapes),
+        in_specs=[anywhere] * len(items),
+        out_specs=tuple([anywhere] * len(items)),
+        scratch_shapes=[sem for shape in shapes for sem in mail_sems(shape.shape[0])],
         compiler_params=pltpu.CompilerParams(collective_id=cid, has_side_effects=True),
         name=name,
-    )(blocks)
+    )(*[x for x, _ in items])
 
 
 def head_lanes(width, head, size):
@@ -600,7 +648,47 @@
     )
 
 
-def attend_kernel(size, block, q_ref, k_ref, v_ref, key_seg_ref, query_seg_ref, mixed_ref, lse_ref):
+def beside_mail(src, out, sems, work):
+    w = place()
+
+    @pl.when(pl.program_id(0) == 0)
+    def _():
+        greet_mail(w, [(HALF, out.shape[0])])
+        mail(w, HALF, src, out, *sems)
+
+    work()
+
+    @pl.when(pl.program_id(0) == pl.num_programs(0) - 1)
+    def _():
+        for cp in mail_copies(w, HALF, src, out, *sems):
+            cp.wait()
+
+
+def attend_kernel(
+    size,
+    block,
+    q_ref,
+    k_ref,
+    v_ref,
+    key_seg_ref,
+    query_seg_ref,
+    mail_ref,
+    mixed_ref,
+    lse_ref,
+    mailed_ref,
+    *sems,
+):
+    beside_mail(
+        mail_ref,
+        mailed_ref,
+        sems,
+        lambda: attend_step(
+            size, block, q_ref, k_ref, v_ref, key_seg_ref, query_seg_ref, mixed_ref, lse_ref
+        ),
+    )
+
+
+def attend_step(size, block, q_ref, k_ref, v_ref, key_seg_ref, query_seg_ref, mixed_ref, lse_ref):
     length, width = q_ref.shape[1:]
     heads = width // size
     scale = size**-0.5
@@ -632,7 +720,7 @@
         mixed_ref[0, rows, :] = jnp.concatenate(parts, axis=0).T
 
 
-def attend(queries, keys, values, segs, size, name):
+def attend(queries, keys, values, segs, letters, size, name, cid):
     count, length, width = queries.shape
     heads = width // size
     whole = pl.BlockSpec((1, length, width), lambda i: (i, 0, 0))
@@ -642,6 +730,7 @@
         out_shape=(
             jax.ShapeDtypeStruct((count, length, width), jnp.float32),
             jax.ShapeDtypeStruct((count, heads, length), jnp.float32),
+            jax.ShapeDtypeStruct(letters.shape, letters.dtype),
         ),
         in_specs=[
             whole,
@@ -649,14 +738,28 @@
             whole,
             pl.BlockSpec((1, length, 1), lambda i: (i, 0, 0)),
             pl.BlockSpec((1, 1, length), lambda i: (i, 0, 0)),
+            pl.BlockSpec(memory_space=pl.ANY),
         ],
-        out_specs=(whole, pl.BlockSpec((1, heads, length), lambda i: (i, 0, 0))),
-        compiler_params=pltpu.CompilerParams(vmem_limit_bytes=48 << 20),
+        out_specs=(
+            whole,
+            pl.BlockSpec((1, heads, length), lambda i: (i, 0, 0)),
+            pl.BlockSpec(memory_space=pl.ANY),
+        ),
+        scratch_shapes=mail_sems(letters.shape[0]),
+        compiler_params=pltpu.CompilerParams(
+            collective_id=cid, has_side_effects=True, vmem_limit_bytes=48 << 20
+        ),
         name=name,
-    )(queries, keys, values, segs[:, :, None], segs[:, None, :])
-
-
-def attend_back_kernel(
+    )(queries, keys, values, segs[:, :, None], segs[:, None, :], letters)
+
+
+def attend_back_kernel(size, block, *refs):
+    mail_ref, mailed_ref = refs[8], refs[12]
+    kept = refs[:8] + refs[9:12] + refs[13:15]
+    beside_mail(mail_ref, mailed_ref, refs[15:], lambda: attend_back_step(size, block, *kept))
+
+
+def attend_back_step(
     size,
     block,
     q_ref,
@@ -716,7 +819,7 @@
     v_back_ref[0] = v_sum[...].astype(jnp.bfloat16)
 
 
-def attend_back(queries, keys, values, back, mixed, lse, segs, size, name):
+def attend_back(queries, keys, values, back, mixed, lse, segs, letters, size, name, cid):
     count, length, width = queries.shape
     heads = width // size
     whole = pl.BlockSpec((1, length, width), lambda i: (i, 0, 0))
@@ -724,18 +827,21 @@
     return pl.pallas_call(
         functools.partial(attend_back_kernel, size, min(256, length)),
         grid=(count,),
-        out_shape=(shape, shape, shape),
+        out_shape=(shape, shape, shape, jax.ShapeDtypeStruct(letters.shape, letters.dtype)),
         in_specs=[whole] * 5
         + [
             pl.BlockSpec((1, heads, length), lambda i: (i, 0, 0)),
             pl.BlockSpec((1, length, 1), lambda i: (i, 0, 0)),
             pl.BlockSpec((1, 1, length), lambda i: (i, 0, 0)),
+            pl.BlockSpec(memory_space=pl.ANY),
         ],
-        out_specs=(whole, whole, whole),
-        scratch_shapes=[pltpu.VMEM((length, width), jnp.float32)] * 2,
-        compiler_params=pltpu.CompilerParams(vmem_limit_bytes=48 << 20),
+        out_specs=(whole, whole, whole, pl.BlockSpec(memory_space=pl.ANY)),
+        scratch_shapes=[pltpu.VMEM((length, width), jnp.float32)] * 2 + mail_sems(letters.shape[0]),
+        compiler_params=pltpu.CompilerParams(
+            collective_id=cid, has_side_effects=True, vmem_limit_bytes=48 << 20
+        ),
         name=name,
-    )(queries, keys, values, back, mixed, lse, segs[:, :, None], segs[:, None, :])
+    )(queries, keys, values, back, mixed, lse, segs[:, :, None], segs[:, None, :], letters)
 
 
 def near_half(blocks, ns, group):
@@ -823,7 +929,13 @@
         down_bias,
         up_bias,
     ]
-    vectors = lax.all_gather(jnp.concatenate(vector_parts), ("dp", "seq"), axis=0)
+    attend_pieces = jnp.concatenate(
+        [pieces(query_weight), pieces(key_weight), pieces(value_weight)], axis=2
+    )
+    letter = jnp.concatenate(vector_parts)
+    letter = jnp.pad(letter, (0, -letter.shape[0] % 2048)).reshape(-1, 128)
+    attend_blocks, vectors = swap([(attend_pieces, HALF), (letter, SPREAD)], "swap_attend", 0)
+    vectors = vectors.reshape(ndev, -1)
     cuts, at = [], 0
     for part in vector_parts:
         cuts.append(vectors[:, at : at + part.shape[0]])
@@ -842,13 +954,12 @@
         ).astype(jnp.float32)
 
     query_shift, value_shift, up_shift = (rank_vector(cuts[i]) for i in (2, 3, 8))
-    attend_pieces = jnp.concatenate(
-        [pieces(query_weight), pieces(key_weight), pieces(value_weight)], axis=2
-    )
-    attend_weight = whole_rows(group_swap(attend_pieces, "swap_attend", 0))
-    output_rows = jnp.concatenate(pair(output_weight, trade(output_weight)))
-    up_columns = whole_rows(group_swap(pieces(up_weight), "swap_up", 1))
-    down_rows = jnp.concatenate(pair(down_weight, trade(down_weight)))
+    attend_weight = whole_rows(attend_blocks)
+    output_trade, down_trade, up_pieces, attend_weight = lax.optimization_barrier(
+        (output_weight, down_weight, pieces(up_weight), attend_weight)
+    )
+    output_rows = jnp.concatenate(pair(output_weight, trade(output_trade)))
+    down_rows = jnp.concatenate(pair(down_weight, trade(down_trade)))
 
     beside_dp = [(d, d + 1 - 2 * (d % 2)) for d in range(nd)]
     other_segs = lax.ppermute(segments, "dp", beside_dp)
@@ -878,7 +989,10 @@
     queries = (pre[:, :take] + query_shift).astype(jnp.bfloat16).reshape(2, -1, take)
     keys = pre[:, take : 2 * take].astype(jnp.bfloat16).reshape(2, -1, take)
     values = (pre[:, 2 * take :] + value_shift).astype(jnp.bfloat16).reshape(2, -1, take)
-    mixed_full, lse = attend(queries, keys, values, segs, size, "attend")
+    mixed_full, lse, up_blocks = attend(
+        queries, keys, values, segs, up_pieces, size, "attend", 1
+    )
+    up_columns = whole_rows(up_blocks)
     mixed = mixed_full.reshape(-1, take).astype(jnp.bfloat16)
     attention = scattered(
         jnp.dot(mixed, output_rows, preferred_element_type=jnp.float32).astype(jnp.bfloat16),
@@ -906,9 +1020,20 @@
     attention_back_own = (keep * middle_back).astype(jnp.bfloat16)
     attention_back = gathered(attention_back_own, "gather_attention_back", 7)
     mixed_back = transposed(attention_back, output_rows).astype(jnp.bfloat16)
-    queries_back, keys_back, values_back = attend_back(
-        queries, keys, values, mixed_back.reshape(2, -1, take), mixed_full, lse, segs, size, "attend_back"
-    )
+    queries_back, keys_back, values_back, up_blocks = attend_back(
+        queries,
+        keys,
+        values,
+        mixed_back.reshape(2, -1, take),
+        mixed_full,
+        lse,
+        segs,
+        up_gradient,
+        size,
+        "attend_back",
+        10,
+    )
+    up_rows = from_pieces(up_blocks, hidden_size // ndev)
     stacked = jnp.concatenate([queries_back, keys_back, values_back], axis=2).reshape(-1, 3 * take)
     normed_one_back = scattered(
         transposed(stacked, attend_weight).astype(jnp.bfloat16), "scatter_normed_one_back", 8
@@ -924,12 +1049,6 @@
     norm_first, pull_one = jax.vjp(layer_norm, inputs, gain_one, shift_one)
     inputs_part, gain_one_sum, shift_one_sum = pull_one(normed_one_back)
     tokens_gradient = (middle_back + inputs_part).astype(jnp.bfloat16)
-
-    up_rows = from_pieces(group_swap(up_gradient, "swap_up_gradient", 10), hidden_size // ndev)
-    attend_rows = group_swap(attend_gradient, "swap_attend_gradient", 11)
-    matrix_rows = [
-        from_pieces(attend_rows[:, :, i * take : (i + 1) * take], size) for i in range(3)
-    ]
 
     def summed(value):
         return jnp.sum(value.astype(jnp.float32), axis=0)
@@ -958,10 +1077,14 @@
     )
     letter = jnp.concatenate([dense, sparse], axis=1)
     letter = jnp.pad(letter, ((0, 0), (0, -letter.shape[1] % 1024))).reshape(ndev, -1, 128)
-    mail = jnp.sum(world_swap(letter, "swap_vectors", 12), axis=0).reshape(-1)
+    attend_rows, mailed = swap([(attend_gradient, HALF), (letter, WORLD)], "swap_last", 11)
+    matrix_rows = [
+        from_pieces(attend_rows[:, :, i * take : (i + 1) * take], size) for i in range(3)
+    ]
+    mailed = jnp.sum(mailed, axis=0).reshape(-1)
     vector_out, at = [], 0
     for part in (share,) * 6 + (size, size, hidden_size // ndev):
-        vector_out.append(mail[at : at + part])
+        vector_out.append(mailed[at : at + part])
         at += part
     (
         gain_one_part,

time: 811 us -> 740 us (0.912)
  blocking collectives: 80.5 us -> 0 us
  waiting for transfers between devices: 0.02 us -> 38.3 us
  Pallas kernels: 530 us -> 512 us
    all_gather x1 -> x0, blocking collectives: 80.5 us -> none  [on_device_halves(): lax.all_gather(jnp.concatenate(vector_parts), ('dp', 'seq'), axis=0)]
    pallas_call x1, Pallas kernels: 7.94 us -> 67.5 us  [attend_back(): pl.pallas_call(functools.partial(attend_back_kernel, size, min(256, lengt...]
    pallas_call x5 -> x2, Pallas kernels: 111 us -> 54.8 us  [swap(): pl.pallas_call(functools.partial(mail_kernel, kinds), out_shape=tuple(sha...]
    pallas_call x4, Pallas kernels: 197 us -> 159 us  [cube_gather(): pl.pallas_call(gather_kernel, out_shape=jax.ShapeDtypeStruct((2, 2, 2, 2,...]
    ppermute x8, waiting for transfers between devices: 0.02 us -> 38.3 us  [trade(): return lax.ppermute(value, 'dp', mirror)]
    pallas_call x4, Pallas kernels: 204 us -> 213 us  [cube_scatter(): pl.pallas_call(scatter_kernel, out_shape=jax.ShapeDtypeStruct((rows, widt...]
    pallas_call x1, Pallas kernels: 9.51 us -> 18 us  [attend(): pl.pallas_call(functools.partial(attend_kernel, size, min(256, length)),...]
    unnamed x144 -> x123, local copies, waits for them, and re-layouts: 23 us -> 20.1 us
  transfers between devices with their start and end apart: 9 -> 9, of which waited for: 0 -> 2; matrix products, arithmetic and copies ran while one was open for 11% -> 10% of each run, Pallas kernels for 49% -> 47%
where the time goes in v2:
time: 740 us; the launch traced here: 734 us
  Pallas kernels  512 us (69%)
  matrix products  80.3 us (11%)
  local copies, waits for them, and re-layouts  49 us (7%)
  waiting for transfers between devices  38.3 us (5%)
  other arithmetic  36.4 us (5%)
  starting transfers between devices  14.8 us (2%)
    pallas_call x4, Pallas kernels, cube_scatter(): pl.pallas_call(scatter_kernel, out_shape=jax.ShapeDtypeStruct((rows, widt...  213 us
    pallas_call x4, Pallas kernels, cube_gather(): pl.pallas_call(gather_kernel, out_shape=jax.ShapeDtypeStruct((2, 2, 2, 2,...  159 us
    pallas_call x1, Pallas kernels, attend_back(): pl.pallas_call(functools.partial(attend_back_kernel, size, min(256, lengt...  67.5 us
    pallas_call x2, Pallas kernels, swap(): pl.pallas_call(functools.partial(mail_kernel, kinds), out_shape=tuple(sha...  54.8 us
    ppermute x8, waiting for transfers between devices, trade(): return lax.ppermute(value, 'dp', mirror)  38.3 us
    dot_general x4, matrix products, transposed(): lax.dot_general(left, right, (((1,), (1,)), ((), ())), preferred_element_...  28.4 us
    dot_general x4, matrix products, leading(): lax.dot_general(left, right, (((0,), (0,)), ((), ())), preferred_element_...  26.6 us
    unnamed x123, local copies, waits for them, and re-layouts  20.1 us
  transfers between devices with their start and end apart: 9, of which 2 were waited for; matrix products, arithmetic and copies ran while one was open for 10% of the time, Pallas kernels for 47%

profile of v2, /device:TPU:0, one launch (start us, length us, event | category | flops | bytes accessed | tf_op | source)
XLA Modules:
  0.0 733.6 jit_solution(11369299596000239450)
XLA Ops:
  0.7 1.5 reshape.381
  8.2 21.1 %swap_attend.1 = (bf16[16,64,384]{2,1,0:T(8,128)(2,1)}, bf16[32,16,128]{2,1,0:T(8,128)(2,1)}) custom-call(bf16[16,64,384]{2,1,0:T(8,128)(2,1)} %pad_maximum_fusion.10.refs_0_, bf16[16,128]{1,0:T(8,128)(2,1)} %pad_bitcast_fusion.1.refs_1_), custom_call_target="tpu_custom_call" | custom-call | tf_op jit(solution)/shard_map/swap_attend/pallas_call | solution.py:623
  29.4 3.4 collective-permute-start
  36.7 1.7 reshape.391.mail_ref
  38.3 44.4 %gather_one.1 = bf16[2,2,2,2,128,2048]{5,4,3,2,1,0:T(8,128)(2,1)S(1)} custom-call(bf16[128,2048]{1,0:T(8,128)(2,1)S(1)} %fusion.18.src), custom_call_target="tpu_custom_call" | custom-call | tf_op jit(solution)/shard_map/gather_one/pallas_call | solution.py:445
  82.8 3.3 copy-done.3
  86.8 2.5 broadcast_select_fusion.5
  89.4 1.3 pad_maximum_fusion.2
  90.7 7.4 %fusion.56 = f32[2048,384]{1,0:T(8,128)S(1)} fusion(bf16[2048,2048]{1,0:T(8,128)(2,1)} %bitcast.185, bf16[2048,384]{1,0:T(8,128)(2,1)S(1)} %pad_maximum_fusion.2), kind=kOutput, calls=%fused_computation.168 | convolution fusion | flops 3221225472 | bytes 13107200 | tf_op jit(solution)/shard_map/dot_general | solution.py:987
  98.2 3.3 collective-permute-start.2
  101.8 18.0 %attend.1 = (f32[2,1024,128]{2,1,0:T(8,128)S(1)}, f32[2,2,1024]{2,1,0:T(2,128)S(1)}, bf16[16,64,512]{2,1,0:T(8,128)(2,1)}) custom-call(bf16[2,1024,128]{2,1,0:T(8,128)(2,1)S(1)} %bitcast.201, bf16[2,1024,128]{2,1,0:T(8,128)(2,1)S(1)} %bitcast.197, bf16[2,1024,128]{2,1,0:T(8,128)(2,1)S(1)} %bitcast.199, s32[2,1024,1]{2,1,0:T(8,128)S(1)} %copy.72.key_seg_ref.refs_6_, ...), custom_call_target="tpu_custom_call" | custom-call | tf_op jit(solution)/shard_map/attend/pallas_call | solution.py:727
  120.5 3.3 collective-permute-start.4
  123.9 2.3 convolution_convert_fusion.3
  126.3 94.7 %scatter_attention.1 = f32[128,2048]{1,0:T(8,128)S(1)} custom-call(bf16[2,2,2,2,128,2048]{5,4,3,2,1,0:T(8,128)(2,1)S(1)} %bitcast.181), custom_call_target="tpu_custom_call" | custom-call | tf_op jit(solution)/shard_map/scatter_attention/pallas_call | solution.py:529
  221.9 37.5 %gather_two.1 = bf16[2,2,2,2,128,2048]{5,4,3,2,1,0:T(8,128)(2,1)S(1)} custom-call(bf16[128,2048]{1,0:T(8,128)(2,1)S(1)} %add_convert_fusion.4.src), custom_call_target="tpu_custom_call" | custom-call | tf_op jit(solution)/shard_map/gather_two/pallas_call | solution.py:445
  259.5 3.2 copy-done.4
  262.7 40.5 %gather_branch_back.1 = bf16[2,2,2,2,128,2048]{5,4,3,2,1,0:T(8,128)(2,1)S(1)} custom-call(bf16[128,2048]{1,0:T(8,128)(2,1)S(1)} %get-tuple-element.59.src), custom_call_target="tpu_custom_call" | custom-call | tf_op jit(solution)/shard_map/gather_branch_back/pallas_call | solution.py:445
  303.3 3.3 copy-done.5
  306.6 2.7 broadcast_select_fusion.3
  310.3 7.6 %fusion.8 = f32[2048,512]{1,0:T(8,128)S(1)} fusion(bf16[2048,2048]{1,0:T(8,128)(2,1)} %bitcast.189, bf16[1024,512]{1,0:T(8,128)(2,1)} %bitcast.223, bf16[1024,512]{1,0:T(8,128)(2,1)} %bitcast.220), kind=kOutput, calls=%fused_computation.30 | convolution fusion | flops 4299161600 | bytes 14680064 | tf_op jit(solution)/shard_map/dot_general | solution.py:1007
  318.0 11.4 %fusion.44 = f32[512,2048]{1,0:T(8,128)} fusion(bf16[2048,2048]{1,0:T(8,128)(2,1)} %bitcast.193, f32[2048,512]{1,0:T(8,128)S(1)} %fusion.8, f32[512]{0:T(512)S(1)} %maximum_convert_fusion), kind=kOutput, calls=%fused_computation.158 | convolution fusion | flops 4305453056 | bytes 16779264 | tf_op jit(solution)/shard_map/dot_general | solution.py:37
  329.4 1.8 broadcast_select_fusion.1
  332.5 9.6 %convert_reduce_fusion = (f32[512]{0:T(512)S(1)}, bf16[2048,512]{1,0:T(8,128)(2,1)}) fusion(f32[2048,512]{1,0:T(8,128)S(1)} %fusion.8, f32[512]{0:T(512)S(1)} %maximum_convert_fusion, bf16[2048,2048]{1,0:T(8,128)(2,1)S(1)} %bitcast.196, bf16[256,2048]{1,0:T(8,128)(2,1)S(1)} %get-tuple-element.71, bf16[256,2048]{1,0:T(8,128)(2,1)S(1)} %get-tuple-element.70), kind=kOutput, calls=%fused_computation.13 | convolution fusion | flops 4323278336 | bytes 16781312 | tf_op jit(solution)/shard_map/dot_general | solution.py:31
  342.1 7.9 %convolution_convert_fusion.2 = bf16[2048,2048]{1,0:T(8,128)(2,1)S(1)} fusion(bf16[256,2048]{1,0:T(8,128)(2,1)} %copy-done.28, bf16[256,2048]{1,0:T(8,128)(2,1)} %copy-done.27, f32[2048,512]{1,0:T(8,128)} %copy-done.48, f32[512]{0:T(512)S(1)} %maximum_convert_fusion), kind=kOutput, calls=%fused_computation.2 | convolution fusion | flops 4313841664 | bytes 14682112 | tf_op jit(solution)/shard_map/dot_general | solution.py:1042
  350.0 7.8 %fusion.57 = f32[2048,512]{1,0:T(8,128)} fusion(bf16[2048,2048]{1,0:T(8,128)(2,1)S(1)} %bitcast.192, bf16[2048,512]{1,0:T(8,128)(2,1)} %get-tuple-element.123), kind=kOutput, calls=%fused_computation.169 | convolution fusion | flops 4294967296 | bytes 14680064 | tf_op jit(solution)/shard_map/dot_general | solution.py:37
  357.8 9.7 %convolution_convert_fusion.1 = bf16[2048,2048]{1,0:T(8,128)(2,1)} fusion(bf16[2048,512]{1,0:T(8,128)(2,1)} %get-tuple-element.123, bf16[1024,512]{1,0:T(8,128)(2,1)} %bitcast.224, bf16[1024,512]{1,0:T(8,128)(2,1)S(1)} %bitcast.221), kind=kOutput, calls=%fused_computation.1 | convolution fusion | flops 4303355904 | bytes 12582912 | tf_op jit(solution)/shard_map/dot_general | solution.py:31
  367.5 39.5 %scatter_branch.1 = f32[128,2048]{1,0:T(8,128)S(1)} custom-call(bf16[2,2,2,2,128,2048]{5,4,3,2,1,0:T(8,128)(2,1)S(1)} %bitcast.183), custom_call_target="tpu_custom_call" | custom-call | tf_op jit(solution)/shard_map/scatter_branch/pallas_call | solution.py:529
  406.9 40.0 %scatter_normed_two_back.1 = f32[128,2048]{1,0:T(8,128)S(1)} custom-call(bf16[2,2,2,2,128,2048]{5,4,3,2,1,0:T(8,128)(2,1)S(1)} %bitcast.184), custom_call_target="tpu_custom_call" | custom-call | tf_op jit(solution)/shard_map/scatter_normed_two_back/pallas_call | solution.py:529
  449.6 36.6 %gather_attention_back.1 = bf16[2,2,2,2,128,2048]{5,4,3,2,1,0:T(8,128)(2,1)S(1)} custom-call(bf16[128,2048]{1,0:T(8,128)(2,1)S(1)} %get-tuple-element.61.src), custom_call_target="tpu_custom_call" | custom-call | tf_op jit(solution)/shard_map/gather_attention_back/pallas_call | solution.py:445
  486.2 2.4 convolution_convert_fusion.4
  492.8 3.8 collective-permute-start.7
  498.0 27.7 %collective-permute-done.7 = bf16[64,2048]{1,0:T(8,128)(2,1)S(1)} collective-permute-done((bf16[64,2048]{1,0:T(8,128)(2,1)}, bf16[64,2048]{1,0:T(8,128)(2,1)S(1)}, u32[]{:S(2)}, u32[]{:S(2)}) %collective-permute-start.7) | collective-permute-done | bytes 262176 | tf_op jit(solution)/shard_map/ppermute | solution.py:884
  526.6 4.2 add_convert_fusion
  530.8 2.4 rev.42
  533.2 2.6 bitcast_select_fusion.refs_8_
  535.8 67.5 %attend_back.1 = (bf16[2,1024,128]{2,1,0:T(8,128)(2,1)S(1)}, bf16[2,1024,128]{2,1,0:T(8,128)(2,1)S(1)}, bf16[2,1024,128]{2,1,0:T(8,128)(2,1)S(1)}, bf16[16,64,512]{2,1,0:T(8,128)(2,1)S(1)}) custom-call(bf16[2,1024,128]{2,1,0:T(8,128)(2,1)S(1)} %bitcast.202, bf16[2,1024,128]{2,1,0:T(8,128)(2,1)S(1)} %bitcast.198, bf16[2,1024,128]{2,1,0:T(8,128)(2,1)S(1)} %bitcast.200, ...), custom_call_target="tpu_custom_call" | custom-call | tf_op jit(solution)/shard_map/attend_back/pallas_call | solution.py:827
  604.1 6.8 convolution_convert_fusion
  611.0 6.2 fusion.58
  617.2 1.3 reshape.432
  618.6 1.9 fusion.50
  620.9 3.4 copy-done.1
  624.3 38.8 %scatter_normed_one_back.1 = f32[128,2048]{1,0:T(8,128)S(1)} custom-call(bf16[2,2,2,2,128,2048]{5,4,3,2,1,0:T(8,128)(2,1)S(1)} %bitcast.182), custom_call_target="tpu_custom_call" | custom-call | tf_op jit(solution)/shard_map/scatter_normed_one_back/pallas_call | solution.py:529
  664.7 1.3 fusion.26
  666.1 1.5 copy.97
  668.6 4.5 convert_add_fusion
  673.0 10.5 %collective-permute-done.6 = bf16[1024,384]{1,0:T(8,128)(2,1)S(1)} collective-permute-done((bf16[1024,384]{1,0:T(8,128)(2,1)S(1)}, bf16[1024,384]{1,0:T(8,128)(2,1)S(1)}, u32[]{:S(2)}, u32[]{:S(2)}) %collective-permute-start.6) | collective-permute-done | bytes 786464 | tf_op jit(solution)/shard_map/ppermute | solution.py:884
  683.6 2.1 add_convert_fusion.1
  686.8 33.7 %swap_last.1 = (bf16[16,64,384]{2,1,0:T(8,128)(2,1)}, f32[32,8,128]{2,1,0:T(8,128)}) custom-call(bf16[16,64,384]{2,1,0:T(8,128)(2,1)} %bitcast_select_fusion.1.refs_0_, f32[32,8,128]{2,1,0:T(8,128)} %bitcast.228), custom_call_target="tpu_custom_call" | custom-call | tf_op jit(solution)/shard_map/swap_last/pallas_call | solution.py:623
  (249 shorter events, 41.2 us)
Async XLA Ops:
  2.3 2.6 copy-start.34
  3.8 2.6 copy-start.38
  3.9 2.6 copy-start.39
  3.9 2.6 copy-start.40
  3.9 2.6 copy-start.41
  3.9 2.6 copy-start.42
  4.6 28.1 %copy-start.37 = (s32[1,1024]{1,0:T(1,128)S(1)}, s32[1,1024]{1,0:T(1,128)}, u32[]{:S(2)}) copy-start(s32[1,1024]{1,0:T(1,128)} %param.20) | copy-start | bytes 12292
  4.9 28.9 %copy-start.29 = (bf16[64,8192]{1,0:T(8,128)(2,1)S(1)}, bf16[64,8192]{1,0:T(8,128)(2,1)}, u32[]{:S(2)}) copy-start(bf16[64,8192]{1,0:T(8,128)(2,1)} %param.33) | copy-start | bytes 3145732
  6.6 27.8 %copy-start.12 = (bf16[1,128,2048]{2,1,0:T(8,128)(2,1)S(1)}, bf16[1,128,2048]{2,1,0:T(8,128)(2,1)}, u32[]{:S(2)}) copy-start(bf16[1,128,2048]{2,1,0:T(8,128)(2,1)} %param.19) | copy-start | bytes 1572868
  29.4 57.4 %collective-permute-start = (bf16[16,64,384]{2,1,0:T(8,128)(2,1)}, bf16[16,64,384]{2,1,0:T(8,128)(2,1)}, u32[]{:S(2)}, u32[]{:S(2)}) collective-permute-start(bf16[16,64,384]{2,1,0:T(8,128)(2,1)} %get-tuple-element.33), channel_id=1, source_target_pairs={{0,24},{8,16},{16,8},{24,0},{1,25},{9,17},{17,9},{25,1},{2,26},{10... | collective-permute-start | bytes 2359304 | tf_op jit(solution)/shard_map/ppermute | solution.py:884
  32.8 53.6 %collective-permute-start.1 = (s32[1,1024]{1,0:T(1,128)S(1)}, s32[1,1024]{1,0:T(1,128)S(1)}, u32[]{:S(2)}, u32[]{:S(2)}) collective-permute-start(s32[1,1024]{1,0:T(1,128)S(1)} %copy-done.37), channel_id=1, source_target_pairs={{0,8},{8,0},{16,24},{24,16},{1,9},{9,1},{17,25},{25,17},{2,10},{10... | collective-permute-start | bytes 12296 | tf_op jit(solution)/shard_map/ppermute | solution.py:965
  38.3 48.4 %copy-start.32 = (bf16[16,64,384]{2,1,0:T(8,128)(2,1)S(1)}, bf16[16,64,384]{2,1,0:T(8,128)(2,1)}, u32[]{:S(2)}) copy-start(bf16[16,64,384]{2,1,0:T(8,128)(2,1)} %get-tuple-element.33) | copy-start | bytes 2359300
  82.8 3.3 copy-start.3
  86.7 15.0 %copy-start = (s32[2,1024,1]{2,1,0:T(8,128)}, s32[2,1024,1]{2,1,0:T(8,128)S(1)}, u32[]{:S(2)}) copy-start(s32[2,1024,1]{2,1,0:T(8,128)S(1)} %copy.72.key_seg_ref.refs_6_) | copy-start | bytes 24580
  90.7 7.5 %copy-start.24 = (bf16[2048,384]{1,0:T(8,128)(2,1)}, bf16[2048,384]{1,0:T(8,128)(2,1)S(1)}, u32[]{:S(2)}) copy-start(bf16[2048,384]{1,0:T(8,128)(2,1)S(1)} %pad_maximum_fusion.2) | copy-start | bytes 4718596
  90.7 7.5 %copy-start.35 = (bf16[64,2048]{1,0:T(8,128)(2,1)S(1)}, bf16[64,2048]{1,0:T(8,128)(2,1)}, u32[]{:S(2)}) copy-start(bf16[64,2048]{1,0:T(8,128)(2,1)} %param.29) | copy-start | bytes 786436
  98.2 3.6 copy-start.8
  98.2 25.6 %collective-permute-start.2 = (bf16[64,2048]{1,0:T(8,128)(2,1)S(1)}, bf16[64,2048]{1,0:T(8,128)(2,1)S(1)}, u32[]{:S(2)}, u32[]{:S(2)}) collective-permute-start(bf16[64,2048]{1,0:T(8,128)(2,1)S(1)} %copy-done.35), channel_id=1, source_target_pairs={{0,24},{8,16},{16,8},{24,0},{1,25},{9,17},{17,9},{25,1},{2,26},{10... | collective-permute-start | bytes 786440 | tf_op jit(solution)/shard_map/ppermute | solution.py:884
  119.8 6.5 copy-start.6
  119.8 186.8 %collective-permute-start.3 = (bf16[16,64,512]{2,1,0:T(8,128)(2,1)}, bf16[16,64,512]{2,1,0:T(8,128)(2,1)}, u32[]{:S(2)}, u32[]{:S(2)}) collective-permute-start(bf16[16,64,512]{2,1,0:T(8,128)(2,1)} %get-tuple-element.38), channel_id=1, source_target_pairs={{0,24},{8,16},{16,8},{24,0},{1,25},{9,17},{17,9},{25,1},{2,26},{10... | collective-permute-start | bytes 3145736 | tf_op jit(solution)/shard_map/ppermute | solution.py:884
  120.5 5.8 copy-start.18
  120.5 208.9 %collective-permute-start.4 = (bf16[256,2048]{1,0:T(8,128)(2,1)}, bf16[256,2048]{1,0:T(8,128)(2,1)}, u32[]{:S(2)}, u32[]{:S(2)}) collective-permute-start(bf16[256,2048]{1,0:T(8,128)(2,1)} %param.35), channel_id=1, source_target_pairs={{0,24},{8,16},{16,8},{24,0},{1,25},{9,17},{17,9},{25,1},{2,26},{10... | collective-permute-start | bytes 3145736 | tf_op jit(solution)/shard_map/ppermute | solution.py:884
  126.3 94.7 %copy-start.21 = (bf16[1,128,2048]{2,1,0:T(8,128)(2,1)S(1)}, bf16[1,128,2048]{2,1,0:T(8,128)(2,1)}, u32[]{:S(2)}) copy-start(bf16[1,128,2048]{2,1,0:T(8,128)(2,1)} %param.37) | copy-start | bytes 1572868
  221.4 38.0 %copy-start.10 = (f32[128,2048]{1,0:T(8,128)}, f32[128,2048]{1,0:T(8,128)S(1)}, u32[]{:S(2)}) copy-start(f32[128,2048]{1,0:T(8,128)S(1)} %get-tuple-element.121) | copy-start | bytes 3145732
  259.4 3.3 copy-start.4
  303.3 3.3 copy-start.5
  310.3 22.2 %slice-start.4 = ((s8[8388608]{0:T(1024)(128)(4,1)}), s8[4194304]{0:T(1024)(128)(4,1)S(1)}, s32[]{:S(2)}) async-start(s8[8388608]{0:T(1024)(128)(4,1)} %bitcast.194), calls=%async_computation.4 | async-start | bytes 8388608
  318.0 13.2 %copy-start.48 = (f32[2048,512]{1,0:T(8,128)}, f32[2048,512]{1,0:T(8,128)S(1)}, u32[]{:S(2)}) copy-start(f32[2048,512]{1,0:T(8,128)S(1)} %fusion.8) | copy-start | bytes 12582916
  318.0 14.5 %slice-start.5 = ((s8[8388608]{0:T(1024)(128)(4,1)}), s8[4194304]{0:T(1024)(128)(4,1)S(1)}, s32[]{:S(2)}) async-start(s8[8388608]{0:T(1024)(128)(4,1)} %bitcast.194), calls=%async_computation.5 | async-start | bytes 8388608
  329.4 20.6 %slice-start.2 = ((s8[8388608]{0:T(1024)(128)(4,1)}), s8[4194304]{0:T(1024)(128)(4,1)S(1)}, s32[]{:S(2)}) async-start(s8[8388608]{0:T(1024)(128)(4,1)} %bitcast.190), calls=%async_computation.2 | async-start | bytes 8388608
  332.5 17.5 %slice-start.3 = ((s8[8388608]{0:T(1024)(128)(4,1)}), s8[4194304]{0:T(1024)(128)(4,1)S(1)}, s32[]{:S(2)}) async-start(s8[8388608]{0:T(1024)(128)(4,1)} %bitcast.190), calls=%async_computation.3 | async-start | bytes 8388608
  350.0 7.8 %copy-start.26 = (bf16[16,64,512]{2,1,0:T(8,128)(2,1)S(1)}, bf16[16,64,512]{2,1,0:T(8,128)(2,1)}, u32[]{:S(2)}) copy-start(bf16[16,64,512]{2,1,0:T(8,128)(2,1)} %get-tuple-element.68) | copy-start | bytes 3145732
  367.4 39.5 %copy-start.2 = (bf16[2048,2048]{1,0:T(8,128)(2,1)S(1)}, bf16[2048,2048]{1,0:T(8,128)(2,1)}, u32[]{:S(2)}) copy-start(bf16[2048,2048]{1,0:T(8,128)(2,1)} %convolution_convert_fusion.1) | copy-start | bytes 25165828
  406.9 40.0 %copy-start.11 = (f32[128,2048]{1,0:T(8,128)S(1)}, f32[128,2048]{1,0:T(8,128)}, u32[]{:S(2)}) copy-start(f32[128,2048]{1,0:T(8,128)} %copy-done.10) | copy-start | bytes 3145732
  449.6 36.6 %copy-start.31 = (bf16[64,2048]{1,0:T(8,128)(2,1)S(1)}, bf16[64,2048]{1,0:T(8,128)(2,1)}, u32[]{:S(2)}) copy-start(bf16[64,2048]{1,0:T(8,128)(2,1)} %copy-done.30) | copy-start | bytes 786436
  488.6 8.0 %copy-start.15 = (f32[512,2048]{1,0:T(8,128)S(1)}, f32[512,2048]{1,0:T(8,128)}, u32[]{:S(2)}) copy-start(f32[512,2048]{1,0:T(8,128)} %fusion.44) | copy-start | bytes 12582916
  492.0 34.6 %collective-permute-start.5 = (bf16[1024,512]{1,0:T(8,128)(2,1)}, bf16[1024,512]{1,0:T(8,128)(2,1)}, u32[]{:S(2)}, u32[]{:S(2)}) collective-permute-start(bf16[1024,512]{1,0:T(8,128)(2,1)} %select_convert_fusion.1), channel_id=1, source_target_pairs={{0,24},{8,16},{16,8},{24,0},{1,25},{9,17},{17,9},{25,1},{2,26},{10... | collective-permute-start | bytes 3145736 | tf_op jit(solution)/shard_map/ppermute | solution.py:884
  492.8 33.0 %collective-permute-start.7 = (bf16[64,2048]{1,0:T(8,128)(2,1)}, bf16[64,2048]{1,0:T(8,128)(2,1)S(1)}, u32[]{:S(2)}, u32[]{:S(2)}) collective-permute-start(bf16[64,2048]{1,0:T(8,128)(2,1)} %select_convert_fusion.3), channel_id=1, source_target_pairs={{0,24},{8,16},{16,8},{24,0},{1,25},{9,17},{17,9},{25,1},{2,26},{10... | collective-permute-start | bytes 786440 | tf_op jit(solution)/shard_map/ppermute | solution.py:884
  497.8 170.8 %collective-permute-start.8 = (bf16[256,2048]{1,0:T(8,128)(2,1)}, bf16[256,2048]{1,0:T(8,128)(2,1)}, u32[]{:S(2)}, u32[]{:S(2)}) collective-permute-start(bf16[256,2048]{1,0:T(8,128)(2,1)} %select_convert_fusion), channel_id=1, source_target_pairs={{0,24},{8,16},{16,8},{24,0},{1,25},{9,17},{17,9},{25,1},{2,26},{10... | collective-permute-start | bytes 3145736 | tf_op jit(solution)/shard_map/ppermute | solution.py:884
  530.8 5.0 copy-start.7
  535.8 68.3 %copy-start.25 = (bf16[2048,384]{1,0:T(8,128)(2,1)S(1)}, bf16[2048,384]{1,0:T(8,128)(2,1)}, u32[]{:S(2)}) copy-start(bf16[2048,384]{1,0:T(8,128)(2,1)} %copy-done.24) | copy-start | bytes 4718596
  535.8 75.1 %slice-start = ((s8[8388608]{0:T(1024)(128)(4,1)}), s8[4194304]{0:T(1024)(128)(4,1)S(1)}, s32[]{:S(2)}) async-start(s8[8388608]{0:T(1024)(128)(4,1)} %bitcast.186), calls=%async_computation | async-start | bytes 8388608
  603.3 7.6 %copy-start.9 = (bf16[16,64,512]{2,1,0:T(8,128)(2,1)}, bf16[16,64,512]{2,1,0:T(8,128)(2,1)S(1)}, u32[]{:S(2)}) copy-start(bf16[16,64,512]{2,1,0:T(8,128)(2,1)S(1)} %get-tuple-element.46) | copy-start | bytes 3145732
  604.1 6.8 slice-start.1
  620.9 3.4 copy-start.1
  624.3 38.8 %copy-start.13 = (bf16[1,128,2048]{2,1,0:T(8,128)(2,1)S(1)}, bf16[1,128,2048]{2,1,0:T(8,128)(2,1)}, u32[]{:S(2)}) copy-start(bf16[1,128,2048]{2,1,0:T(8,128)(2,1)} %param.19) | copy-start | bytes 1572868
  624.3 39.7 %copy-start.20 = (f32[2048,384]{1,0:T(8,128)S(1)}, f32[2048,384]{1,0:T(8,128)}, u32[]{:S(2)}) copy-start(f32[2048,384]{1,0:T(8,128)} %fusion.58) | copy-start | bytes 9437188
  664.2 19.4 %collective-permute-start.6 = (bf16[1024,384]{1,0:T(8,128)(2,1)S(1)}, bf16[1024,384]{1,0:T(8,128)(2,1)S(1)}, u32[]{:S(2)}, u32[]{:S(2)}) collective-permute-start(bf16[1024,384]{1,0:T(8,128)(2,1)S(1)} %select_convert_fusion.2), channel_id=1, source_target_pairs={{0,24},{8,16},{16,8},{24,0},{1,25},{9,17},{17,9},{25,1},{2,26},{10... | collective-permute-start | bytes 2359304 | tf_op jit(solution)/shard_map/ppermute | solution.py:884
  (16 other events, 31.4 us)

commit v3 on v0

--- a/solution.py
+++ b/solution.py
@@ -1,8 +1,11 @@
+import functools
 import math
 
 import jax
 import jax.numpy as jnp
 from jax import lax
+from jax.experimental import pallas as pl
+from jax.experimental.pallas import tpu as pltpu
 from jax.sharding import PartitionSpec as P
 
 HEADS = 32
@@ -367,6 +370,1160 @@
     )
 
 
+MESH = pl.DeviceIdType.MESH
+ORDERS = ("xyz", "yzx", "zxy")
+CANON = "zyx"
+ALL = (pl.ds(0, 2),) * 3
+SLICE_IN, SLICE_OUT, WORLD, SPREAD, PAIR, NEAR = range(6)
+VMEM_BYTES = 56 << 20
+
+
+def place():
+    d, s = lax.axis_index("dp"), lax.axis_index("seq")
+    half = lax.axis_size("dp") // 2
+    far = d // half
+    z = d + far * (2 * half - 1 - 2 * d)
+    return dict(d=d, s=s, g=far, z=z, y=s // 4, x=(s // 2) % 2, c=s % 2)
+
+
+def beside(w, dim):
+    if dim == "z":
+        return (w["d"] + 1 - 2 * (w["d"] % 2), w["s"])
+    step = {"c": 1, "x": 2, "y": 4}[dim]
+    return (w["d"], w["s"] + step * (1 - 2 * w[dim]))
+
+
+def partner(w):
+    return (lax.axis_size("dp") - 1 - w["d"], w["s"])
+
+
+def peer(w, r):
+    n = lax.axis_size("seq")
+    e, s = r // n, r % n
+    return (e + w["g"] * (lax.axis_size("dp") - 1 - 2 * e), s)
+
+
+def row_block(w, r):
+    n = lax.axis_size("seq")
+    e, s = r // n, r % n
+    return (e + w["g"] * (1 - 2 * e)) * n + s
+
+
+def anyone(i):
+    n = lax.axis_size("seq")
+    return (i // n, i % n)
+
+
+def half_peers(w):
+    count = lax.axis_size("dp") * lax.axis_size("seq") // 2
+    me = w["z"] * lax.axis_size("seq") + w["s"]
+    return me, [(me + k) % count for k in range(1, count)]
+
+
+def world_peers(w):
+    count = lax.axis_size("dp") * lax.axis_size("seq")
+    me = w["d"] * lax.axis_size("seq") + w["s"]
+    return me, [(me + k) % count for k in range(1, count)]
+
+
+def greet(ids):
+    bar = pltpu.get_barrier_semaphore()
+    for i in ids:
+        pl.semaphore_signal(bar, inc=1, device_id=i, device_id_type=MESH)
+    pl.semaphore_wait(bar, len(ids))
+
+
+def greet_half(w):
+    greet([peer(w, r) for r in half_peers(w)[1]] + [partner(w)])
+
+
+def greet_world(w):
+    greet([anyone(i) for i in world_peers(w)[1]])
+
+
+def remote(src, dst, send, recv, device):
+    return pltpu.make_async_remote_copy(
+        src_ref=src,
+        dst_ref=dst,
+        send_sem=send,
+        recv_sem=recv,
+        device_id=device,
+        device_id_type=MESH,
+    )
+
+
+def mail(w, kind, src, out, send, recv, local):
+    if kind == SLICE_IN:
+        me, others = half_peers(w)
+        todo = [(src.at[r], peer(w, r)) for r in others]
+        own, to = src.at[me], out.at[row_block(w, me)]
+    elif kind == SLICE_OUT:
+        me, others = half_peers(w)
+        todo = [(src.at[row_block(w, r)], peer(w, r)) for r in others]
+        own, to = src.at[row_block(w, me)], out.at[me]
+    elif kind == WORLD:
+        me, others = world_peers(w)
+        todo = [(src.at[i], anyone(i)) for i in others]
+        own, to = src.at[me], out.at[me]
+    elif kind == SPREAD:
+        me, others = world_peers(w)
+        todo = [(src, anyone(i)) for i in others]
+        own, to = src, out.at[me]
+    elif kind == PAIR:
+        todo, own, to = [(src, partner(w))], src, out.at[w["g"]]
+    else:
+        todo, own, to = [(src, beside(w, "z"))], src, out.at[w["z"]]
+    copies = [
+        remote(part, to, send.at[k], recv.at[k], device) for k, (part, device) in enumerate(todo)
+    ]
+    return copies + [pltpu.make_async_copy(own, to, local)]
+
+
+def start_all(copies):
+    for cp in copies:
+        cp.start()
+
+
+def wait_all(copies):
+    for cp in copies:
+        cp.wait()
+
+
+def mail_count(kind):
+    count = lax.axis_size("dp") * lax.axis_size("seq")
+    return {SLICE_IN: count // 2, SLICE_OUT: count // 2, WORLD: count, SPREAD: count}.get(kind, 2)
+
+
+def mail_sems(kind):
+    n = mail_count(kind) - 1
+    dma = pltpu.SemaphoreType.DMA
+    return [dma((n,)), dma((n,)), dma]
+
+
+def mail_shape(kind, x):
+    if kind in (SPREAD, PAIR, NEAR):
+        return jax.ShapeDtypeStruct((mail_count(kind),) + x.shape, x.dtype)
+    return jax.ShapeDtypeStruct(x.shape, x.dtype)
+
+
+def mail_kernel(kinds, *refs):
+    n = len(kinds)
+    srcs, outs, sems = refs[:n], refs[n : 2 * n], refs[2 * n :]
+    w = place()
+    greet_world(w)
+    copies = []
+    for i, kind in enumerate(kinds):
+        copies += mail(w, kind, srcs[i], outs[i], *sems[3 * i : 3 * i + 3])
+    start_all(copies)
+    wait_all(copies)
+
+
+def exchange(items, name, cid):
+    anywhere = pl.BlockSpec(memory_space=pl.ANY)
+    kinds = [kind for _, kind in items]
+    return pl.pallas_call(
+        functools.partial(mail_kernel, kinds),
+        out_shape=tuple(mail_shape(kind, x) for x, kind in items),
+        in_specs=[anywhere] * len(items),
+        out_specs=tuple([anywhere] * len(items)),
+        scratch_shapes=[sem for kind in kinds for sem in mail_sems(kind)],
+        compiler_params=pltpu.CompilerParams(collective_id=cid, has_side_effects=True),
+        name=name,
+    )(*[x for x, _ in items])
+
+
+def column_parts(width):
+    unit = width // 128
+    third = unit // 3
+    parts, at = [], 0
+    for count in (unit - 2 * third, third, third):
+        parts.append(pl.ds(at * 128, count * 128))
+        at += count
+    return parts
+
+
+def box(w, both, other=()):
+    return tuple(
+        pl.ds(0, 2) if q in both else (1 - w[q] if q in other else w[q]) for q in CANON
+    )
+
+
+class Gather:
+    def __init__(self, w, src, out, send, recv, side_send, side_recv, local):
+        self.w, self.src, self.out = w, src, out
+        self.send, self.recv, self.side_send, self.side_recv = send, recv, side_send, side_recv
+        self.parts = column_parts(src.shape[1])
+        self.own = (w["z"], w["y"], w["x"], w["c"])
+        self.keep = pltpu.make_async_copy(src, out.at[self.own], local)
+        self.links, self.sides = {}, []
+
+    @staticmethod
+    def sems():
+        dma = pltpu.SemaphoreType.DMA
+        return [dma((3, 3)), dma((3, 3)), dma((3, 4)), dma((3, 4)), dma]
+
+    def push(self, p, k, src, dst):
+        cp = remote(
+            src, dst, self.send.at[p, k], self.recv.at[p, k], beside(self.w, ORDERS[p][k])
+        )
+        cp.start()
+        self.links[p, k] = cp
+
+    def across(self, p, k, src, dst):
+        cp = remote(
+            src, dst, self.side_send.at[p, k], self.side_recv.at[p, k], beside(self.w, "c")
+        )
+        cp.start()
+        self.sides.append(cp)
+
+    def start(self):
+        for p, cols in enumerate(self.parts):
+            self.push(p, 0, self.src.at[:, cols], self.out.at[self.own + (slice(None), cols)])
+        self.keep.start()
+        for p, cols in enumerate(self.parts):
+            self.across(p, 0, self.src.at[:, cols], self.out.at[self.own + (slice(None), cols)])
+
+    def step(self, k):
+        w = self.w
+        if k == 0:
+            self.keep.wait()
+        for p, cols in enumerate(self.parts):
+            order = ORDERS[p]
+            self.links[p, k].wait_recv()
+            tail = (w["c"], slice(None), cols)
+            if k < 2:
+                held = self.out.at[box(w, order[: k + 1]) + tail]
+                self.push(p, k + 1, held, held)
+            new = self.out.at[box(w, order[:k], order[k]) + tail]
+            self.across(p, k + 1, new, new)
+
+    def finish(self):
+        for cp in self.links.values():
+            cp.wait_send()
+        wait_all(self.sides)
+
+
+class Scatter:
+    def __init__(self, w, acc, away, side, land, send, recv, side_send, side_recv):
+        self.w, self.acc, self.away, self.side, self.land = w, acc, away, side, land
+        self.send, self.recv, self.side_send, self.side_recv = send, recv, side_send, side_recv
+        self.parts = column_parts(acc.shape[-1])
+        self.links, self.sides = {}, {}
+
+    @staticmethod
+    def scratch(rows, width):
+        most = column_parts(width)[0].size
+        half = pltpu.VMEM((2, 2, 2, rows, width), jnp.bfloat16)
+        dma = pltpu.SemaphoreType.DMA
+        return [
+            half,
+            half,
+            half,
+            pltpu.VMEM((3, 2, 2, rows, most), jnp.bfloat16),
+            pltpu.VMEM((3, 2, rows, most), jnp.bfloat16),
+            pltpu.VMEM((3, rows, most), jnp.bfloat16),
+            dma((3, 3)),
+            dma((3, 3)),
+            dma((3,)),
+            dma((3,)),
+        ]
+
+    @staticmethod
+    def over(w, refs):
+        return Scatter(w, *refs[:3], refs[3:6], *refs[6:])
+
+    def produce(self, p, product):
+        w, cols = self.w, self.parts[p]
+        rows = self.acc.shape[3]
+
+        def fill(out, core):
+            @pl.loop(0, 4)
+            def _(i):
+                block = product(i // 2, i % 2, core, cols)
+                out[i // 2, i % 2, :, :, cols] = block.astype(out.dtype).reshape(2, rows, -1)
+
+        fill(self.away, 1 - w["c"])
+        at = ALL + (slice(None), cols)
+        cp = remote(
+            self.away.at[at],
+            self.side.at[at],
+            self.side_send.at[p],
+            self.side_recv.at[p],
+            beside(w, "c"),
+        )
+        cp.start()
+        self.sides[p] = cp
+        fill(self.acc, w["c"])
+
+    def at(self, order, k, other, rest):
+        w = self.w
+        left = dict(zip([q for q in CANON if q in order[k + 1 :]], rest))
+        here = {q: w[q] for q in order[:k]}
+        here[order[k]] = 1 - w[order[k]] if other else w[order[k]]
+        here.update(left)
+        return tuple(here[q] for q in CANON)
+
+    def add(self, at, got, cols):
+        at = at + (slice(None), cols)
+        total = self.acc[at].astype(jnp.float32) + got.astype(jnp.float32)
+        self.acc[at] = total.astype(self.acc.dtype)
+
+    def push(self, p, k):
+        w, cols, order = self.w, self.parts[p], ORDERS[p]
+        src = self.acc.at[box(w, order[k + 1 :], order[k]) + (slice(None), cols)]
+        dst = self.land[k].at[
+            (p,) + (pl.ds(0, 2),) * (2 - k) + (slice(None), pl.ds(0, cols.size))
+        ]
+        cp = remote(src, dst, self.send.at[p, k], self.recv.at[p, k], beside(w, order[k]))
+        cp.start()
+        self.links[p, k] = cp
+
+    def fold(self, p):
+        cols, order = self.parts[p], ORDERS[p]
+        self.sides[p].wait_recv()
+
+        def add(other):
+            @pl.loop(0, 4)
+            def _(i):
+                at = self.at(order, 0, other, (i // 2, i % 2))
+                self.add(at, self.side[at + (slice(None), cols)], cols)
+
+        add(True)
+        self.push(p, 0)
+        add(False)
+
+    def step(self, k):
+        w = self.w
+        for p, cols in enumerate(self.parts):
+            order = ORDERS[p]
+            self.links[p, k].wait_recv()
+            left = [q for q in CANON if q in order[k + 1 :]]
+            slot = left.index(order[k + 1])
+            inner = (slice(None), pl.ds(0, cols.size))
+            for other in (True, False):
+                here = 1 - w[order[k + 1]] if other else w[order[k + 1]]
+                if k == 0:
+
+                    @pl.loop(0, 2)
+                    def _(i):
+                        rest = (here, i) if slot == 0 else (i, here)
+                        got = self.land[0][(p,) + rest + inner]
+                        self.add(self.at(order, 0, False, rest), got, cols)
+
+                else:
+                    got = self.land[1][(p, here) + inner]
+                    self.add(self.at(order, 1, False, (here,)), got, cols)
+                if other:
+                    self.push(p, k + 1)
+
+    def finish(self, out):
+        w = self.w
+        own = (w["z"], w["y"], w["x"])
+        for p, cols in enumerate(self.parts):
+            self.links[p, 2].wait_recv()
+            got = self.land[2][p, :, pl.ds(0, cols.size)]
+            out[:, cols] = self.acc[own + (slice(None), cols)].astype(jnp.float32) + got.astype(
+                jnp.float32
+            )
+        for cp in self.links.values():
+            cp.wait_send()
+        for cp in self.sides.values():
+            cp.wait_send()
+
+
+def across(left, right):
+    return lax.dot_general(
+        left, right, (((1,), (1,)), ((), ())), preferred_element_type=jnp.float32
+    )
+
+
+def straight(left, right):
+    return jnp.dot(left, right, preferred_element_type=jnp.float32)
+
+
+def flat(block):
+    return block.reshape(-1, block.shape[-1])
+
+
+def head_lanes(width, head, size):
+    lane = lax.broadcasted_iota(jnp.int32, (1, width), 1)
+    return jnp.logical_and(lane >= head * size, lane < (head + 1) * size)
+
+
+def used_pairs(key_seg, query_seg, first, length, block):
+    key_pos = lax.broadcasted_iota(jnp.int32, (length, 1), 0)
+    query_pos = first + lax.broadcasted_iota(jnp.int32, (1, block), 1)
+    return jnp.logical_and(key_seg == query_seg, key_pos <= query_pos)
+
+
+def attend_block(size, block, first, q, k, v_flip, key_seg, query_seg, mixed, mixed_low, lse):
+    width = q.shape[2]
+    upto, rows = first + block, pl.ds(first, block)
+
+    @pl.loop(0, q.shape[0])
+    def _(i):
+        allowed = used_pairs(key_seg[i, pl.ds(0, upto), :], query_seg[i, :, rows], first, upto, block)
+        keys = k[i, pl.ds(0, upto), :]
+        query = q[i, rows, :] * jnp.asarray(size**-0.5, q.dtype)
+        parts = []
+        for head in range(width // size):
+            own = jnp.where(head_lanes(width, head, size), query, jnp.zeros_like(query))
+            scores = jnp.where(allowed, across(keys, own), NEG)
+            top = jnp.max(scores, axis=0, keepdims=True)
+            weights = jnp.exp(scores - top)
+            total = jnp.sum(weights, axis=0, keepdims=True)
+            lse[i, pl.ds(head, 1), rows] = top + jnp.log(total)
+            probs = (weights * (1.0 / total)).astype(q.dtype)
+            parts.append(straight(v_flip[i, pl.ds(head * size, size), pl.ds(0, upto)], probs))
+        full = jnp.concatenate(parts, axis=0).T
+        mixed[i, rows, :] = full
+        at = first // block
+        mixed_low[i, at // 2, at % 2] = full.astype(mixed_low.dtype).reshape(mixed_low.shape[3:])
+
+
+def attend_back_block(
+    size, block, first, q, k, k_flip, v, back, mixed, lse, key_seg, query_seg, q_back, k_sum, v_sum
+):
+    width = q.shape[2]
+    upto, rows = first + block, pl.ds(first, block)
+    before = pl.ds(0, upto)
+    scale = size**-0.5
+
+    @pl.loop(0, q.shape[0])
+    def _(i):
+        allowed = used_pairs(key_seg[i, before, :], query_seg[i, :, rows], first, upto, block)
+        keys, values = k[i, before, :], v[i, before, :]
+        query = q[i, rows, :] * jnp.asarray(scale, q.dtype)
+        grad = back[i, rows, :]
+        product = (grad.astype(jnp.float32) * mixed[i, rows, :]).T
+        parts = []
+        for head in range(width // size):
+            lanes = head_lanes(width, head, size)
+            own = jnp.where(lanes, query, jnp.zeros_like(query))
+            own_grad = jnp.where(lanes, grad, jnp.zeros_like(grad))
+            delta = jnp.sum(product[head * size : (head + 1) * size, :], axis=0, keepdims=True)
+            scores = across(keys, own) - lse[i, pl.ds(head, 1), rows]
+            probs = jnp.exp(jnp.where(allowed, scores, NEG))
+            score_back = (probs * (across(values, own_grad) - delta)).astype(q.dtype)
+            v_sum[i, before, :] += straight(probs.astype(q.dtype), own_grad)
+            k_sum[i, before, :] += straight(score_back, own)
+            parts.append(straight(k_flip[i, pl.ds(head * size, size), before], score_back))
+        q_back[i, rows, :] = (jnp.concatenate(parts, axis=0).T * scale).astype(q_back.dtype)
+
+
+class Refs:
+    def __init__(self, refs):
+        self.refs, self.used = refs, 0
+
+    def take(self, count):
+        self.used += count
+        return self.refs[self.used - count : self.used]
+
+
+def attend_kernel(size, *refs):
+    refs = Refs(refs)
+    (own, grad, shift, out_rows, key_seg, query_seg, blocks, pieces, down) = refs.take(9)
+    (attention, q, k, v, mixed, lse, rows_all, grads_all, pair, columns, downs) = refs.take(11)
+    rows, grads, weight, v_flip, mixed_low = refs.take(5)
+    one = refs.take(5)
+    two = refs.take(5)
+    sums = refs.take(10)
+    pair_sems, column_sems, down_sems = refs.take(3), refs.take(3), refs.take(3)
+    load, flush = refs.take(2)
+    w = place()
+    greet_half(w)
+    gather = Gather(w, own, rows, *one)
+    second = Gather(w, grad, grads, *two)
+    scatter = Scatter.over(w, sums)
+    gather.start()
+    pair_mail = mail(w, PAIR, blocks, pair, *pair_sems)
+    start_all(pair_mail)
+    gather.step(0)
+    column_mail = mail(w, SLICE_IN, pieces, columns, *column_sems)
+    start_all(column_mail)
+    gather.step(1)
+    gather.step(2)
+    wait_all(pair_mail)
+    fetch = [
+        pltpu.make_async_copy(pair.at[i], weight.at[pl.ds(i * pair.shape[1], pair.shape[1])], load.at[i])
+        for i in range(2)
+    ]
+    start_all(fetch)
+    gather.finish()
+    keep_rows = pltpu.make_async_copy(rows, rows_all, flush.at[0])
+    keep_rows.start()
+    down_mail = mail(w, PAIR, down, downs, *down_sems)
+    start_all(down_mail)
+    second.start()
+    wait_all(fetch)
+    length, take = q.shape[1:]
+
+    @pl.loop(0, 4)
+    def _(i):
+        block = straight(flat(rows[i // 2, i % 2]), weight[...]) + shift[...]
+        at = pl.ds(i % 2 * (length // 2), length // 2)
+        for ref, n in ((q, 0), (k, 1), (v, 2)):
+            ref[i // 2, at, :] = block[:, n * take : (n + 1) * take].astype(ref.dtype)
+        v_flip[i // 2, :, at] = block[:, 2 * take :].astype(v_flip.dtype).T
+
+    second.step(0)
+    block = length // 4
+    for first in range(0, length, block):
+        attend_block(
+            size, block, first, q, k, v_flip, key_seg, query_seg, mixed, mixed_low, lse
+        )
+        if first == block:
+            second.step(1)
+
+    def product(e, y, c, cols):
+        return straight(flat(mixed_low[e, y, :, c]), out_rows[:, cols])
+
+    for p in range(3):
+        scatter.produce(p, product)
+    second.step(2)
+    for p in range(3):
+        scatter.fold(p)
+    second.finish()
+    keep_grads = pltpu.make_async_copy(grads, grads_all, flush.at[1])
+    keep_grads.start()
+    scatter.step(0)
+    scatter.step(1)
+    scatter.finish(attention)
+    wait_all(down_mail)
+    wait_all(column_mail)
+    keep_rows.wait()
+    keep_grads.wait()
+
+
+def attend(own, grad, shift, out_rows, segs, blocks, pieces, down, size, name, cid):
+    rows, width = own.shape
+    ns = lax.axis_size("seq")
+    length = rows * ns
+    take = out_rows.shape[0]
+    low, f32 = own.dtype, jnp.float32
+    vmem, anywhere = pl.BlockSpec(memory_space=pltpu.VMEM), pl.BlockSpec(memory_space=pl.ANY)
+    shape, dma = jax.ShapeDtypeStruct, pltpu.SemaphoreType.DMA
+    whole = (2, 2, 2, 2, rows, width)
+    return pl.pallas_call(
+        functools.partial(attend_kernel, size),
+        out_shape=(
+            shape((rows, width), f32),
+            *[shape((2, length, take), low)] * 3,
+            shape((2, length, take), f32),
+            shape((2, take // size, length), f32),
+            shape(whole, low),
+            shape(whole, low),
+            shape((2,) + blocks.shape, low),
+            shape(pieces.shape, low),
+            shape((2,) + down.shape, low),
+        ),
+        in_specs=[vmem] * 6 + [anywhere] * 3,
+        out_specs=tuple([vmem] * 6 + [anywhere] * 5),
+        scratch_shapes=[
+            pltpu.VMEM(whole, low),
+            pltpu.VMEM(whole, low),
+            pltpu.VMEM((2 * blocks.shape[0], blocks.shape[1]), low),
+            pltpu.VMEM((2, take, length), low),
+            pltpu.VMEM((2, 2, 2, 2, rows, take), low),
+            *Gather.sems(),
+            *Gather.sems(),
+            *Scatter.scratch(rows, width),
+            *mail_sems(PAIR),
+            *mail_sems(SLICE_IN),
+            *mail_sems(PAIR),
+            dma((2,)),
+            dma((2,)),
+        ],
+        compiler_params=pltpu.CompilerParams(
+            collective_id=cid, has_side_effects=True, vmem_limit_bytes=VMEM_BYTES
+        ),
+        name=name,
+    )(own, grad, shift, out_rows, segs[:, :, None], segs[:, None, :], blocks, pieces, down)
+
+
+def feed_kernel(*refs):
+    refs = Refs(refs)
+    own, shift, columns, grads_all, downs = refs.take(5)
+    back, hidden, shift_sum, down_grad, up_grad = refs.take(5)
+    rows, grads, up, down, hidden_flip, pre_flip, pre = refs.take(7)
+    one = refs.take(5)
+    sums = refs.take(10)
+    up_send, up_recv, up_local = refs.take(3)
+    (load,) = refs.take(1)
+    w = place()
+    greet_half(w)
+    gather = Gather(w, own, rows, *one)
+    scatter = Scatter.over(w, sums)
+    gather.start()
+    half = columns.shape[0]
+    mine = up.at[pl.ds(w["g"] * half, half)]
+    trade = remote(columns, mine, up_send, up_recv, partner(w))
+    keep = pltpu.make_async_copy(columns, mine, up_local)
+    fetch = [
+        pltpu.make_async_copy(downs, down, load.at[0]),
+        pltpu.make_async_copy(grads_all, grads, load.at[1]),
+    ]
+    start_all([trade, keep] + fetch)
+    for k in range(3):
+        gather.step(k)
+    gather.finish()
+    wait_all([trade, keep] + fetch)
+    width = down.shape[1]
+    span = rows.shape[2] * rows.shape[3] * rows.shape[4]
+    shift_sum[...] = jnp.zeros_like(shift_sum)
+
+    @pl.loop(0, 4)
+    def _(i):
+        before = straight(flat(rows[i // 2, i % 2]), up[...]) + shift[...]
+        active, pull = jax.vjp(activate, before)
+        at = pl.ds(i * span, span)
+        low = active.astype(hidden.dtype)
+        hidden[i // 2, i % 2] = low.reshape(hidden.shape[2:])
+        hidden_flip[:, at] = low.T
+        hidden_back = across(flat(grads[i // 2, i % 2]), down[...])
+        pre_back = pull(hidden_back)[0].astype(pre.dtype)
+        pre[i // 2, i % 2] = pre_back.reshape(pre.shape[2:])
+        pre_flip[:, at] = pre_back.T
+        shift_sum[...] += jnp.sum(pre_back.astype(jnp.float32), axis=0, keepdims=True)
+
+    def product(e, y, c, cols):
+        return across(flat(pre[e, y, :, c]), up[cols, :])
+
+    for p in range(3):
+        scatter.produce(p, product)
+    for p in range(3):
+        scatter.fold(p)
+    chunk = 256
+
+    @pl.loop(0, width // chunk)
+    def _(i):
+        cols = pl.ds(i * chunk, chunk)
+        grad = straight(hidden_flip[...], grads[:, :, :, :, :, cols].reshape(-1, chunk))
+        down_grad[:, cols] = grad.astype(down_grad.dtype)
+
+    scatter.step(0)
+
+    @pl.loop(0, width // chunk)
+    def _(i):
+        cols = pl.ds(i * chunk, chunk)
+        grad = straight(pre_flip[...], rows[:, :, :, :, :, cols].reshape(-1, chunk))
+        up_grad[cols, :] = grad.astype(up_grad.dtype).T
+
+    scatter.step(1)
+    scatter.finish(back)
+
+
+def feed(own, shift, columns, grads_all, downs, name, cid):
+    rows, width = own.shape
+    take = columns.shape[1]
+    low, f32 = own.dtype, jnp.float32
+    vmem, anywhere = pl.BlockSpec(memory_space=pltpu.VMEM), pl.BlockSpec(memory_space=pl.ANY)
+    shape, dma = jax.ShapeDtypeStruct, pltpu.SemaphoreType.DMA
+    whole = (2, 2, 2, 2, rows, width)
+    tokens = 16 * rows
+    return pl.pallas_call(
+        feed_kernel,
+        out_shape=(
+            shape((rows, width), f32),
+            shape((2, 2, 2, 2, rows, take), low),
+            shape((1, take), f32),
+            shape((take, width), low),
+            shape((width, take), low),
+        ),
+        in_specs=[vmem] * 2 + [anywhere] * 3,
+        out_specs=tuple([vmem] * 5),
+        scratch_shapes=[
+            pltpu.VMEM(whole, low),
+            pltpu.VMEM(whole, low),
+            pltpu.VMEM((width, take), low),
+            pltpu.VMEM((take, width), low),
+            pltpu.VMEM((take, tokens), low),
+            pltpu.VMEM((take, tokens), low),
+            pltpu.VMEM((2, 2, 2, 2, rows, take), low),
+            *Gather.sems(),
+            *Scatter.scratch(rows, width),
+            dma,
+            dma,
+            dma,
+            dma((2,)),
+        ],
+        compiler_params=pltpu.CompilerParams(
+            collective_id=cid, has_side_effects=True, vmem_limit_bytes=VMEM_BYTES
+        ),
+        name=name,
+    )(own, shift, columns, grads_all, downs)
+
+
+def attend_back_kernel(size, *refs):
+    refs = Refs(refs)
+    (own, out_rows, q, k, v, mixed, lse, key_seg, query_seg) = refs.take(9)
+    rows_all, pair, down_sent, up_sent = refs.take(4)
+    (back, out_grad, attend_grad, q_sum, v_bias_sum, down_got, up_got) = refs.take(7)
+    (grads, rows, weight, k_flip, mixed_flip, grad_heads, q_back, k_sum, v_sum, stack, stack_flip) = (
+        refs.take(11)
+    )
+    one = refs.take(5)
+    sums = refs.take(10)
+    down_send, down_recv, up_send, up_recv = refs.take(4)
+    (load,) = refs.take(1)
+    w = place()
+    greet_half(w)
+    gather = Gather(w, own, grads, *one)
+    scatter = Scatter.over(w, sums)
+    gather.start()
+    down_trade = remote(down_sent.at[1 - w["g"]], down_got, down_send, down_recv, partner(w))
+    up_trade = remote(up_sent.at[1 - w["g"]], up_got, up_send, up_recv, partner(w))
+    down_trade.start()
+    half = pair.shape[1]
+    fetch = [
+        pltpu.make_async_copy(pair.at[i], weight.at[pl.ds(i * half, half)], load.at[i])
+        for i in range(2)
+    ] + [pltpu.make_async_copy(rows_all, rows, load.at[2])]
+    start_all(fetch)
+    length, take = q.shape[1:]
+    for i in range(2):
+        k_flip[i] = k[i].T
+        mixed_flip[:, pl.ds(i * length, length)] = mixed[i].astype(mixed_flip.dtype).T
+    k_sum[...] = jnp.zeros_like(k_sum)
+    v_sum[...] = jnp.zeros_like(v_sum)
+    for step in range(3):
+        gather.step(step)
+    gather.finish()
+
+    @pl.loop(0, 4)
+    def _(i):
+        at = pl.ds(i % 2 * (length // 2), length // 2)
+        grad = across(flat(grads[i // 2, i % 2]), out_rows[...])
+        grad_heads[i // 2, at, :] = grad.astype(grad_heads.dtype)
+
+    block = length // 4
+    for first in range(0, length, block):
+        attend_back_block(
+            size,
+            block,
+            first,
+            q,
+            k,
+            k_flip,
+            v,
+            grad_heads,
+            mixed,
+            lse,
+            key_seg,
+            query_seg,
+            q_back,
+            k_sum,
+            v_sum,
+        )
+    down_trade.wait()
+    up_trade.start()
+    q_sum[...] = jnp.zeros_like(q_sum)
+    v_bias_sum[...] = jnp.zeros_like(v_bias_sum)
+
+    @pl.loop(0, 4)
+    def _(i):
+        at = pl.ds(i % 2 * (length // 2), length // 2)
+        parts = [
+            ref[i // 2, at, :].astype(stack.dtype) for ref in (q_back, k_sum, v_sum)
+        ]
+        for n, part in enumerate(parts):
+            stack[i // 2, i % 2, :, :, :, pl.ds(n * take, take)] = part.reshape(
+                stack.shape[2:5] + (take,)
+            )
+            stack_flip[pl.ds(n * take, take), pl.ds(i * (length // 2), length // 2)] = part.T
+        q_sum[...] += jnp.sum(parts[0].astype(jnp.float32), axis=0, keepdims=True)
+        v_bias_sum[...] += jnp.sum(parts[2].astype(jnp.float32), axis=0, keepdims=True)
+
+    wait_all(fetch)
+
+    def product(e, y, c, cols):
+        return across(flat(stack[e, y, :, c]), weight[cols, :])
+
+    for p in range(3):
+        scatter.produce(p, product)
+    for p in range(3):
+        scatter.fold(p)
+    chunk = 256
+
+    @pl.loop(0, weight.shape[0] // chunk)
+    def _(i):
+        cols = pl.ds(i * chunk, chunk)
+        grad = straight(stack_flip[...], rows[:, :, :, :, :, cols].reshape(-1, chunk))
+        attend_grad[cols, :] = grad.astype(attend_grad.dtype).T
+        grad = straight(mixed_flip[...], grads[:, :, :, :, :, cols].reshape(-1, chunk))
+        out_grad[:, cols] = grad.astype(out_grad.dtype)
+
+    scatter.step(0)
+    scatter.step(1)
+    scatter.finish(back)
+    up_trade.wait()
+
+
+def attend_back(
+    own, out_rows, q, k, v, mixed, lse, segs, rows_all, pair, down_sent, up_sent, size, name, cid
+):
+    rows, width = own.shape
+    length, take = q.shape[1:]
+    low, f32 = own.dtype, jnp.float32
+    vmem, anywhere = pl.BlockSpec(memory_space=pltpu.VMEM), pl.BlockSpec(memory_space=pl.ANY)
+    shape, dma = jax.ShapeDtypeStruct, pltpu.SemaphoreType.DMA
+    whole = (2, 2, 2, 2, rows, width)
+    heads = (2, length, take)
+    return pl.pallas_call(
+        functools.partial(attend_back_kernel, size),
+        out_shape=(
+            shape((rows, width), f32),
+            shape((take, width), low),
+            shape((width, 3 * take), low),
+            shape((1, take), f32),
+            shape((1, take), f32),
+            shape(down_sent.shape[1:], low),
+            shape(up_sent.shape[1:], low),
+        ),
+        in_specs=[vmem] * 9 + [anywhere] * 4,
+        out_specs=tuple([vmem] * 5 + [anywhere] * 2),
+        scratch_shapes=[
+            pltpu.VMEM(whole, low),
+            pltpu.VMEM(whole, low),
+            pltpu.VMEM((width, 3 * take), low),
+            pltpu.VMEM((2, take, length), low),
+            pltpu.VMEM((take, 2 * length), low),
+            pltpu.VMEM(heads, low),
+            pltpu.VMEM(heads, low),
+            pltpu.VMEM(heads, f32),
+            pltpu.VMEM(heads, f32),
+            pltpu.VMEM((2, 2, 2, 2, rows, 3 * take), low),
+            pltpu.VMEM((3 * take, 2 * length), low),
+            *Gather.sems(),
+            *Scatter.scratch(rows, width),
+            dma,
+            dma,
+            dma,
+            dma,
+            dma((3,)),
+        ],
+        compiler_params=pltpu.CompilerParams(
+            collective_id=cid, has_side_effects=True, vmem_limit_bytes=VMEM_BYTES
+        ),
+        name=name,
+    )(
+        own,
+        out_rows,
+        q,
+        k,
+        v,
+        mixed,
+        lse,
+        segs[:, :, None],
+        segs[:, None, :],
+        rows_all,
+        pair,
+        down_sent,
+        up_sent,
+    )
+
+
+def branch_kernel(*refs):
+    refs = Refs(refs)
+    hidden, downs, blocks, attend_sent, out_sent = refs.take(5)
+    branch, swapped, attend_got, out_got = refs.take(4)
+    sums = refs.take(10)
+    swap_sems = refs.take(3)
+    attend_send, attend_recv, out_send, out_recv = refs.take(4)
+    w = place()
+    greet_half(w)
+    scatter = Scatter.over(w, sums)
+    attend_trade = remote(
+        attend_sent.at[1 - w["g"]], attend_got, attend_send, attend_recv, partner(w)
+    )
+    out_trade = remote(out_sent.at[1 - w["g"]], out_got, out_send, out_recv, partner(w))
+    attend_trade.start()
+
+    def product(e, y, c, cols):
+        return straight(flat(hidden[e, y, :, c]), downs[:, cols])
+
+    for p in range(3):
+        scatter.produce(p, product)
+    for p in range(3):
+        scatter.fold(p)
+    copies = mail(w, SLICE_OUT, blocks, swapped, *swap_sems)
+    start_all(copies)
+    scatter.step(0)
+    scatter.step(1)
+    out_trade.start()
+    scatter.finish(branch)
+    attend_trade.wait()
+    out_trade.wait()
+    wait_all(copies)
+
+
+def branch_sum(hidden, downs, blocks, attend_sent, out_sent, name, cid):
+    rows, width = hidden.shape[4], downs.shape[1]
+    vmem, anywhere = pl.BlockSpec(memory_space=pltpu.VMEM), pl.BlockSpec(memory_space=pl.ANY)
+    shape, dma = jax.ShapeDtypeStruct, pltpu.SemaphoreType.DMA
+    return pl.pallas_call(
+        branch_kernel,
+        out_shape=(
+            shape((rows, width), jnp.float32),
+            shape(blocks.shape, blocks.dtype),
+            shape(attend_sent.shape[1:], attend_sent.dtype),
+            shape(out_sent.shape[1:], out_sent.dtype),
+        ),
+        in_specs=[vmem] * 2 + [anywhere] * 3,
+        out_specs=tuple([vmem] + [anywhere] * 3),
+        scratch_shapes=[
+            *Scatter.scratch(rows, width),
+            *mail_sems(SLICE_OUT),
+            dma,
+            dma,
+            dma,
+            dma,
+        ],
+        compiler_params=pltpu.CompilerParams(
+            collective_id=cid, has_side_effects=True, vmem_limit_bytes=VMEM_BYTES
+        ),
+        name=name,
+    )(hidden, downs, blocks, attend_sent, out_sent)
+
+
+def on_device_halves(
+    tokens,
+    segments,
+    exit_layer,
+    first_gain,
+    first_shift,
+    query_weight,
+    query_bias,
+    key_weight,
+    value_weight,
+    value_bias,
+    output_weight,
+    output_bias,
+    second_gain,
+    second_shift,
+    up_weight,
+    up_bias,
+    down_weight,
+    down_bias,
+    cotangent,
+):
+    rows, width = tokens.shape[1:]
+    nd, ns = lax.axis_size("dp"), lax.axis_size("seq")
+    ndev, ranks = nd * ns, nd * ns // 2
+    size = width // HEADS
+    hidden_size = up_weight.shape[1]
+    take = 2 * size
+    w = place()
+    group = w["g"]
+    low_at = w["z"] * ns + w["s"]
+    high_at = (nd - 1 - w["z"]) * ns + w["s"]
+
+    def pieces(weight):
+        cut = weight.reshape(weight.shape[0], 2, 2, ns, -1)
+        both = jnp.stack([cut[:, 0], cut[:, 1, ::-1]], axis=3)
+        return both.transpose(1, 2, 0, 3, 4).reshape(ranks, weight.shape[0], -1)
+
+    def from_pieces(blocks, take):
+        cut = blocks.reshape(2, ns, blocks.shape[1], 2, take)
+        both = jnp.stack([cut[:, :, :, 0], cut[::-1, :, :, 1]]).transpose(3, 0, 1, 2, 4)
+        return both.reshape(blocks.shape[1], -1).astype(jnp.float32)
+
+    def own_half(pair):
+        return lax.dynamic_index_in_dim(pair, group, 0, keepdims=False).astype(jnp.float32)
+
+    def total(pair, got):
+        return own_half(pair) + got.astype(jnp.float32)
+
+    vector_parts = [
+        first_gain,
+        first_shift,
+        query_bias,
+        value_bias,
+        output_bias,
+        second_gain,
+        second_shift,
+        down_bias,
+        up_bias,
+    ]
+    attend_pieces = jnp.concatenate(
+        [pieces(query_weight), pieces(key_weight), pieces(value_weight)], axis=2
+    )
+    letter = jnp.concatenate(vector_parts)
+    letter = jnp.pad(letter, (0, -letter.shape[0] % 2048)).reshape(-1, 128)
+    attend_blocks, vectors, output_rows, segs = exchange(
+        [
+            (attend_pieces, SLICE_IN),
+            (letter, SPREAD),
+            (output_weight, PAIR),
+            (segments.reshape(-1, 128), NEAR),
+        ],
+        "exchange_first",
+        0,
+    )
+    vectors = vectors.reshape(ndev, -1)
+    output_rows = output_rows.reshape(-1, width)
+    segs = segs.reshape(2, -1)
+    cuts, at = [], 0
+    for part in vector_parts:
+        cuts.append(vectors[:, at : at + part.shape[0]])
+        at += part.shape[0]
+    full = [cut.reshape(-1).astype(jnp.float32) for cut in cuts]
+    gain_one, shift_one, _, _, output_shift, gain_two, shift_two, down_shift, _ = full
+
+    def rank_vector(cut):
+        return jnp.concatenate(
+            [
+                lax.dynamic_index_in_dim(cut, low_at, 0, keepdims=False),
+                lax.dynamic_index_in_dim(cut, high_at, 0, keepdims=False),
+            ]
+        ).astype(jnp.float32)
+
+    query_shift, value_shift, up_shift = (rank_vector(cuts[i]) for i in (2, 3, 8))
+    attend_shift = jnp.concatenate([query_shift, jnp.zeros_like(query_shift), value_shift])[None]
+
+    keep = (exit_layer > LAYER).astype(jnp.float32).reshape(rows, 1)
+    inputs = tokens.astype(jnp.float32).reshape(rows, width)
+    upstream = cotangent.astype(jnp.float32).reshape(rows, width)
+    branch_back = (keep * upstream).astype(jnp.bfloat16)
+    normed_one = layer_norm(inputs, gain_one, shift_one).astype(jnp.bfloat16)
+    (
+        attention,
+        queries,
+        keys,
+        values,
+        mixed,
+        lse,
+        normed_all,
+        branch_back_all,
+        attend_pair,
+        up_blocks,
+        down_pair,
+    ) = attend(
+        normed_one,
+        branch_back,
+        attend_shift,
+        output_rows,
+        segs,
+        attend_blocks.reshape(-1, 3 * take),
+        pieces(up_weight),
+        down_weight,
+        size,
+        "attend",
+        1,
+    )
+    middle = inputs + keep * (attention + output_shift)
+    normed_two = layer_norm(middle, gain_two, shift_two).astype(jnp.bfloat16)
+    down_rows = down_pair.reshape(-1, width)
+    normed_two_back, hidden, up_shift_sum, down_grad, up_grad = feed(
+        normed_two,
+        up_shift[None],
+        up_blocks.reshape(width // 2, -1),
+        branch_back_all,
+        down_rows,
+        "feed",
+        2,
+    )
+    norm_result, pull_two = jax.vjp(layer_norm, middle, gain_two, shift_two)
+    middle_part, gain_two_sum, shift_two_sum = pull_two(normed_two_back)
+    middle_back = upstream + middle_part
+    attention_back = (keep * middle_back).astype(jnp.bfloat16)
+    down_grad = down_grad.reshape(2, -1, width)
+    up_grad = up_grad.reshape(2, width // 2, -1)
+    normed_one_back, output_grad, attend_grad, query_sum, value_sum, down_got, up_got = attend_back(
+        attention_back,
+        output_rows,
+        queries,
+        keys,
+        values,
+        mixed,
+        lse,
+        segs,
+        normed_all,
+        attend_pair,
+        down_grad,
+        up_grad,
+        size,
+        "attend_back",
+        3,
+    )
+    up_half = total(up_grad, up_got).astype(jnp.bfloat16).reshape(ranks, width // ndev, -1)
+    attend_grad = attend_grad.reshape(2, width // 2, -1)
+    output_grad = output_grad.reshape(2, -1, width)
+    branch, up_swapped, attend_got, output_got = branch_sum(
+        hidden, down_rows, up_half, attend_grad, output_grad, "branch_sum", 4
+    )
+    layer_out = (middle + keep * (branch + down_shift)).astype(jnp.bfloat16)
+    attend_half = total(attend_grad, attend_got).astype(jnp.bfloat16)
+    attend_half = attend_half.reshape(ranks, width // ndev, -1)
+    norm_first, pull_one = jax.vjp(layer_norm, inputs, gain_one, shift_one)
+    inputs_part, gain_one_sum, shift_one_sum = pull_one(normed_one_back)
+    tokens_gradient = (middle_back + inputs_part).astype(jnp.bfloat16)
+
+    def summed(value):
+        return jnp.sum(value.astype(jnp.float32), axis=0)
+
+    own_sums = [
+        gain_one_sum,
+        shift_one_sum,
+        gain_two_sum,
+        shift_two_sum,
+        summed(attention_back),
+        summed(branch_back),
+    ]
+    share = width // ndev
+    dense = jnp.concatenate([value.reshape(ndev, share) for value in own_sums], axis=1)
+    rank_sums = jnp.concatenate(
+        [query_sum.reshape(2, -1), value_sum.reshape(2, -1), up_shift_sum.reshape(2, -1)], axis=1
+    )
+    number = jnp.arange(ndev)[:, None]
+    sparse = jnp.where(
+        number == low_at, rank_sums[0], jnp.where(number == high_at, rank_sums[1], 0.0)
+    )
+    letter = jnp.concatenate([dense, sparse], axis=1)
+    letter = jnp.pad(letter, ((0, 0), (0, -letter.shape[1] % 1024))).reshape(ndev, -1, 128)
+    attend_swapped, mailed = exchange(
+        [(attend_half, SLICE_OUT), (letter, WORLD)], "exchange_last", 5
+    )
+    matrix_rows = [
+        from_pieces(attend_swapped[:, :, i * take : (i + 1) * take], size) for i in range(3)
+    ]
+    mailed = jnp.sum(mailed, axis=0).reshape(-1)
+    vector_out, at = [], 0
+    for part in (share,) * 6 + (size, size, hidden_size // ndev):
+        vector_out.append(mailed[at : at + part])
+        at += part
+    (
+        gain_one_part,
+        shift_one_part,
+        gain_two_part,
+        shift_two_part,
+        output_shift_part,
+        down_shift_part,
+        query_shift_part,
+        value_shift_part,
+        up_shift_part,
+    ) = vector_out
+    return (
+        layer_out.reshape(tokens.shape),
+        tokens_gradient.reshape(tokens.shape),
+        gain_one_part,
+        shift_one_part,
+        matrix_rows[0],
+        query_shift_part,
+        matrix_rows[1],
+        matrix_rows[2],
+        value_shift_part,
+        total(output_grad, output_got),
+        output_shift_part,
+        gain_two_part,
+        shift_two_part,
+        from_pieces(up_swapped, hidden_size // ndev),
+        up_shift_part,
+        total(down_grad, down_got),
+        down_shift_part,
+    )
+
+
 def solution(mesh):
     placed = (
         P("dp", "seq", None),
@@ -389,8 +1546,9 @@
         P(("dp", "seq")),
         P("dp", "seq", None),
     )
+    halves = mesh.shape["dp"] == 4 and mesh.shape["seq"] == 8
     return jax.shard_map(
-        on_device,
+        on_device_halves if halves else on_device,
         mesh=mesh,
         in_specs=placed,
         out_specs=(

time: 3820 us -> 606 us (0.16)
  waiting for transfers between devices: 3170 us -> 0 us
  Pallas kernels: 0 us -> 524 us
  matrix products: 307 us -> 0 us
  blocking collectives: 100 us -> 0 us
  other arithmetic: 109 us -> 27.2 us
  local copies, waits for them, and re-layouts: 99.3 us -> 45.9 us
    unnamed x15 -> x0, waiting for transfers between devices: 1870 us -> none
    reduce_scatter x1 -> x0, waiting for transfers between devices: 698 us -> none  [on_device(): lax.psum_scatter(leading(hidden, branch_back), ('dp', 'seq'), scatter_dim...]
    all_gather x10 -> x0, waiting for transfers between devices: 606 us -> none  [the longest x1 191 us: on_device(): lax.all_gather(up_weight, ('dp', 'seq'), axis=0, tiled=True)]
    pallas_call x0 -> x6, Pallas kernels: none -> 524 us  [the longest x1 157 us: attend(): pl.pallas_call(functools.partial(attend_kernel, size), out_shape=(shape((...]
    dot_general x72 -> x0, matrix products: 307 us -> none  [the longest x4 77.8 us: leading(): lax.dot_general(left, right, (((0,), (0,)), ((), ())), preferred_element_...]
    concatenate x2 -> x3, other arithmetic: 88.1 us -> 1.07 us  [the longest x1 0.99 us: on_device_halves(): jnp.concatenate([pieces(query_weight), pieces(key_weight), pieces(value_w...]
    all_gather x3 -> x0, blocking collectives: 57.1 us -> none  [the longest x1 39.2 us: on_device(): lax.all_gather(up_bias, ('dp', 'seq'), axis=0, tiled=True)]
    unnamed x1 -> x0, blocking collectives: 43 us -> none
  transfers between devices with their start and end apart: 13 -> 0, of which waited for: 10 -> 0; matrix products, arithmetic and copies ran while one was open for 10% -> 0% of each run, Pallas kernels for 0% -> 0%
where the time goes in v3:
time: 606 us; the launch traced here: 599 us
  Pallas kernels  524 us (86%)
  local copies, waits for them, and re-layouts  45.9 us (8%)
  other arithmetic  27.2 us (4%)
    pallas_call x1, Pallas kernels, attend(): pl.pallas_call(functools.partial(attend_kernel, size), out_shape=(shape((...  157 us
    pallas_call x1, Pallas kernels, attend_back(): pl.pallas_call(functools.partial(attend_back_kernel, size), out_shape=(sh...  130 us
    pallas_call x1, Pallas kernels, feed(): pl.pallas_call(feed_kernel, out_shape=(shape((rows, width), f32), shape((...  120 us
    pallas_call x1, Pallas kernels, branch_sum(): pl.pallas_call(branch_kernel, out_shape=(shape((rows, width), jnp.float32...  69.3 us
    pallas_call x2, Pallas kernels, exchange(): pl.pallas_call(functools.partial(mail_kernel, kinds), out_shape=tuple((ma...  47 us

profile of v3, /device:TPU:0, one launch (start us, length us, event | category | flops | bytes accessed | tf_op | source)
XLA Modules:
  0.0 598.5 jit_solution(7364564162970119760)
XLA Ops:
  0.7 1.5 reshape.328
  6.5 1.0 pad_maximum_fusion.refs_0_
  8.2 27.0 %exchange_first.1 = (bf16[16,64,384]{2,1,0:T(8,128)(2,1)}, bf16[32,16,128]{2,1,0:T(8,128)(2,1)}, bf16[2,64,2048]{2,1,0:T(8,128)(2,1)}, s32[2,8,128]{2,1,0:T(8,128)}) custom-call(bf16[16,64,384]{2,1,0:T(8,128)(2,1)} %pad_maximum_fusion.refs_0_, bf16[16,128]{1,0:T(8,128)(2,1)} %pad_bitcast_fusion.1.refs_1_, bf16[64,2048]{1,0:T(8,128)(2,1)} %refs_2_.1, ...), custom_call_target="tpu_custom_call" | custom-call | tf_op jit(solution)/shard_map/exchange_first/pallas_call | solution.py:524
  35.2 0.9 copy.106
  37.6 1.2 convert_reduce_fusion.1
  38.8 1.8 broadcast_in_dim_reshape.10.refs_4_.refs_7_
  41.2 1.1 copy.69
  42.3 1.7 reshape.342.refs_7_
  43.9 157.5 %attend.1 = (f32[128,2048]{1,0:T(8,128)}, bf16[2,1024,128]{2,1,0:T(8,128)(2,1)}, bf16[2,1024,128]{2,1,0:T(8,128)(2,1)}, bf16[2,1024,128]{2,1,0:T(8,128)(2,1)}, f...) custom-call(bf16[128,2048]{1,0:T(8,128)(2,1)} %get-tuple-element.143, ...), custom_call_target="tpu_custom_call" | custom-call | tf_op jit(solution)/shard_map/attend/pallas_call | solution.py:907
  201.5 1.5 fusion.29
  203.5 1.1 add_convert_fusion.2.refs_0_
  205.1 120.2 %feed.1 = (f32[128,2048]{1,0:T(8,128)}, bf16[2,2,2,2,128,512]{5,4,3,2,1,0:T(8,128)(2,1)}, f32[1,512]{1,0:T(1,128)}, bf16[512,2048]{1,0:T(8,128)(2,1)}, bf16[2048,512]{1,0:T(8,128)(2,1)}) custom-call(bf16[128,2048]{1,0:T(8,128)(2,1)} %add_convert_fusion.2.refs_0_, f32[1,512]{1,0:T(1,128)} %maximum_convert_fusion.refs_1_, bf16[1024,512]{1,0:T(8,128)(2,1)} %bitcast.175, ...), custom_call_target="tpu_custom_call" | custom-call | tf_op jit(solution)/shard_map/feed/pallas_call | solution.py:1024
  325.3 1.7 multiply_reduce_fusion
  327.5 1.0 copy-done.2
  328.5 1.1 convert_reduce_fusion.2
  329.5 129.7 %attend_back.1 = (f32[128,2048]{1,0:T(8,128)}, bf16[128,2048]{1,0:T(8,128)(2,1)}, bf16[2048,384]{1,0:T(8,128)(2,1)}, f32[1,128]{1,0:T(1,128)}, f32[1,128]{1,0:T(...) custom-call(bf16[128,2048]{1,0:T(8,128)(2,1)} %get-tuple-element.95.refs_0_, bf16[128,2048]{1,0:T(8,128)(2,1)} %bitcast.170, ...), custom_call_target="tpu_custom_call" | custom-call | tf_op jit(solution)/shard_map/attend_back/pallas_call | solution.py:1172
  459.2 3.4 convert_add_fusion
  462.6 1.3 fusion
  463.9 69.3 %branch_sum.1 = (f32[128,2048]{1,0:T(8,128)}, bf16[16,64,512]{2,1,0:T(8,128)(2,1)}, bf16[1024,384]{1,0:T(8,128)(2,1)}, bf16[64,2048]{1,0:T(8,128)(2,1)}) custom-call(bf16[2,2,2,2,128,512]{5,4,3,2,1,0:T(8,128)(2,1)} %get-tuple-element.58.refs_0_, bf16[512,2048]{1,0:T(8,128)(2,1)} %bitcast.158, bf16[16,64,512]{2,1,0:T(8,128)(2,1)} %bitcast.164, ...), custom_call_target="tpu_custom_call" | custom-call | tf_op jit(solution)/shard_map/branch_sum/pallas_call | solution.py:1264
  533.3 1.3 reshape.367
  534.6 1.9 fusion.31
  537.0 1.5 copy.95
  538.5 0.8 convert_add_fusion.4
  542.2 0.7 select_select_fusion
  543.2 1.0 fusion.12
  544.4 0.7 reshape.354
  545.0 0.7 reshape.357
  545.7 0.7 reshape.355
  546.4 0.7 reshape.356
  547.1 0.7 reshape.358
  547.7 1.0 concatenate.38
  548.7 0.7 copy.94
  549.4 2.2 fusion.1
  551.6 20.0 %exchange_last.1 = (bf16[16,64,384]{2,1,0:T(8,128)(2,1)}, f32[32,8,128]{2,1,0:T(8,128)}) custom-call(bf16[16,64,384]{2,1,0:T(8,128)(2,1)} %bitcast.168, f32[32,8,128]{2,1,0:T(8,128)} %bitcast.181), custom_call_target="tpu_custom_call" | custom-call | tf_op jit(solution)/shard_map/exchange_last/pallas_call | solution.py:524
  571.6 1.9 fusion.32
  573.6 1.2 reshape.366
  574.8 1.1 fusion.33
  576.2 1.6 copy.80
  577.7 2.4 reshape.381
  580.1 1.2 reshape.365
  581.3 1.1 fusion.34
  582.7 1.6 copy.77
  584.3 2.4 reshape.380
  586.9 1.1 fusion.35
  588.4 1.6 copy.74
  590.0 2.4 reshape.379
  593.6 2.5 fusion.17
  596.2 2.2 fusion.16
  (156 shorter events, 14.1 us)
Async XLA Ops:
  2.2 1.0 copy-start.11
  3.7 1.0 copy-start.12
  5.4 2.1 copy-start.24
  5.4 2.1 copy-start.25
  5.4 2.0 copy-start.26
  5.4 2.0 copy-start.27
  5.4 2.0 copy-start.28
  5.5 2.0 copy-start.29
  5.5 2.0 copy-start.30
  5.5 2.0 copy-start.31
  5.5 2.0 copy-start.32
  6.2 31.0 %copy-start = (bf16[1,128,2048]{2,1,0:T(8,128)(2,1)S(1)}, bf16[1,128,2048]{2,1,0:T(8,128)(2,1)}, u32[]{:S(2)}) copy-start(bf16[1,128,2048]{2,1,0:T(8,128)(2,1)} %param.19) | copy-start | bytes 1572868
  6.4 31.2 %copy-start.33 = (s32[1,128]{1,0:T(1,128)S(1)}, s32[1,128]{1,0:T(1,128)}, u32[]{:S(2)}) copy-start(s32[1,128]{1,0:T(1,128)} %param.21) | copy-start | bytes 1540
  6.5 31.2 %copy-start.4 = (bf16[1,128,2048]{2,1,0:T(8,128)(2,1)S(1)}, bf16[1,128,2048]{2,1,0:T(8,128)(2,1)}, u32[]{:S(2)}) copy-start(bf16[1,128,2048]{2,1,0:T(8,128)(2,1)} %param.37) | copy-start | bytes 1572868
  35.2 3.6 copy-start.15
  37.1 3.6 copy-start.8
  37.6 505.6 %copy-start.16 = (f32[128]{0:T(128)}, f32[128]{0:T(128)S(1)}, u32[]{:S(2)}) copy-start(f32[128]{0:T(128)S(1)} %fusion.23) | copy-start | bytes 1540
  325.3 1.7 copy-start.6
  327.5 1.0 copy-start.2
  327.5 131.7 %copy-start.21 = (f32[128]{0:T(128)}, f32[128]{0:T(128)S(1)}, u32[]{:S(2)}) copy-start(f32[128]{0:T(128)S(1)} %negate_multiply_fusion.1) | copy-start | bytes 1540
  459.2 3.4 copy-start.3
  459.2 3.4 copy-start.9
  537.0 1.6 copy-start.7
  537.0 1.6 copy-start.13
  537.0 2.9 copy-start.35
  537.0 3.6 copy-start.34
  537.0 4.4 copy-start.20
  537.0 5.9 copy-start.1
  539.4 10.0 %copy-start.10 = (bf16[1024,384]{1,0:T(8,128)(2,1)S(1)}, bf16[1024,384]{1,0:T(8,128)(2,1)}, u32[]{:S(2)}) copy-start(bf16[1024,384]{1,0:T(8,128)(2,1)} %get-tuple-element.74) | copy-start | bytes 2359300
  543.2 1.1 copy-start.18
  588.3 4.0 copy-start.14
  588.3 5.2 copy-start.23
  588.3 5.2 copy-start.5
  588.3 5.2 copy-start.17
  588.4 5.2 copy-start.19
  588.4 5.2 copy-start.22
